TPU v7x, 256 devices: a whole 4x4x8 slice. The times are simulated.
256 devices in a mesh: wide: 64 (over z, x_lo, y), narrow: 4 (over x_hi, core).
Axes of the slice: x: 4 (x_hi: 2, x_lo: 2; x = x_hi * 2 + x_lo), y: 4, z: 8, core: 2. Of those that a mesh axis runs over, the one named last changes fastest.
Arguments:
- amplitudes: bfloat16 [24576, 8192], P(None, ('wide', 'narrow')), may hold values from -6 to 6
- integrals: bfloat16 [8192, 4096], P('wide', 'narrow'), may hold values from -0.0625 to 0.0625
- old_residual: float32 [24576, 4096], P('wide', 'narrow'), may hold values from -6 to 6
Outputs:
- new_residual: float32 [24576, 4096], P('wide', 'narrow')
All inputs are finite; a program needn't handle non-finite values.
Results may differ from a plain program's by a relative error of at most 0.0003.
Values may be sent and summed in bfloat16 or wider, within the bound.
No kernel may reach another device: no remote copies, remote signals or barrier semaphores. Data moves between devices by JAX's collectives and lax.ppermute only.
A program may use at most 128 MiB of HBM per device.

v0:
```python
import jax
import jax.numpy as jnp
from jax import lax
from jax.sharding import PartitionSpec as P


def broadcast(value, axis, source):
    kept = jnp.where(lax.axis_index(axis) == source, value, 0).astype(value.dtype)
    return lax.psum(kept, axis)


def per_device(amplitudes, integrals, old_residual):
    panels = lax.axis_size("narrow")
    sub_rows = integrals.shape[0] // panels
    stacked = integrals.reshape(panels, sub_rows, integrals.shape[1])
    total = old_residual
    row_amps = lax.all_to_all(amplitudes, "wide", split_axis=0, concat_axis=1, tiled=True)
    for column in range(panels):
        panel = broadcast(row_amps, "narrow", column)
        panel_ints = lax.all_gather(stacked[column], "wide", axis=0, tiled=True)
        total = total + jnp.dot(panel, panel_ints, preferred_element_type=jnp.float32)
    return total


def solution(mesh):
    placed = (P(None, ("wide", "narrow")), P("wide", "narrow"), P("wide", "narrow"))
    return jax.shard_map(
        per_device, mesh=mesh, in_specs=placed, out_specs=P("wide", "narrow"), check_vma=False
    )
```

profile of v0, /device:TPU:24, one launch (start us, length us, event | category | flops | bytes accessed | tf_op | source)
XLA Modules:
  0.0 1299.3 jit_solution(12446308555164644119)
XLA Ops:
  7.4 0.0 all-gather.5.cloned.1.call-start
  7.4 1.6 fusion
  9.0 0.0 all-gather.5.cloned.1.call-update
  9.0 2.7 copy.11
  11.8 12.8 all-to-all-start
  24.6 0.0 all-reduce.3.cloned.1.call-start
  24.6 40.1 %all-to-all-done = bf16[64,384,32]{1,2,0:T(8,128)(2,1)S(1)} async-done(((bf16[64,384,32]{1,2,0:T(8,128)(2,1)}), bf16[64,384,32]{1,2,0:T(8,128)(2,1)S(1)}, u32[]{:S(2)}, u32[]{:S(2)}) %all-to-all-start) | async-done | bytes 1572896 | tf_op jit(solution)/shard_map/all_to_all | solution.py:17
  64.7 2.9 broadcast_select_fusion
  67.5 0.0 all-reduce.3.cloned.1.call-update
  67.6 0.0 all-gather.7.cloned.1.call-start
  67.6 0.7 all-gather.7.cloned.1.call-update
  68.3 0.0 all-gather.9.cloned.1.call-start
  68.4 0.7 all-gather.9.cloned.1.call-update
  69.1 0.0 all-gather.11.cloned.1.call-start
  69.1 0.5 all-gather.11.cloned.1.call-update
  69.6 303.3 %all-gather.5.cloned.1.call-done = bf16[2048,1024]{1,0:T(8,128)(2,1)} async-done(((bf16[32,1024]{1,0:T(8,128)(2,1)}), bf16[2048,1024]{1,0:T(8,128)(2,1)}) %all-gather.5.cloned.1.call-update) | async-done | bytes 4194320 | tf_op jit(solution)/shard_map/all_gather | solution.py:20
  372.9 5.7 fusion.1
  378.7 301.1 %all-gather.7.cloned.1.call-done = bf16[2048,1024]{1,0:T(8,128)(2,1)} async-done(((bf16[32,1024]{1,0:T(8,128)(2,1)}), bf16[2048,1024]{1,0:T(8,128)(2,1)}) %all-gather.7.cloned.1.call-update) | async-done | bytes 4194320 | tf_op jit(solution)/shard_map/all_gather | solution.py:20
  679.7 5.2 fusion.2
  684.9 297.8 %all-gather.9.cloned.1.call-done = bf16[2048,1024]{1,0:T(8,128)(2,1)} async-done(((bf16[32,1024]{1,0:T(8,128)(2,1)}), bf16[2048,1024]{1,0:T(8,128)(2,1)}) %all-gather.9.cloned.1.call-update) | async-done | bytes 4194320 | tf_op jit(solution)/shard_map/all_gather | solution.py:20
  982.8 5.8 fusion.3
  988.5 297.1 %all-gather.11.cloned.1.call-done = bf16[2048,1024]{1,0:T(8,128)(2,1)} async-done(((bf16[32,1024]{1,0:T(8,128)(2,1)}), bf16[2048,1024]{1,0:T(8,128)(2,1)}) %all-gather.11.cloned.1.call-update) | async-done | bytes 4194320 | tf_op jit(solution)/shard_map/all_gather | solution.py:20
  1285.6 0.0 copy-done
  1285.6 6.6 add_add_fusion
  (6 shorter events, 0.0 us)
Async XLA Ops:
  7.4 365.6 %all-gather.5.cloned.1.call-start = ((), (), s32[]{:S(2)}) async-start(), calls=%async_computation.1 | async-start | bytes 4259840 | tf_op jit(solution)/shard_map/all_gather | solution.py:20
  11.8 52.9 %all-to-all-start = ((bf16[64,384,32]{1,2,0:T(8,128)(2,1)}), bf16[64,384,32]{1,2,0:T(8,128)(2,1)S(1)}, u32[]{:S(2)}, u32[]{:S(2)}) async-start(bf16[64,384,32]{1,2,0:T(8,128)(2,1)} %bitcast.23), calls=%async_computation | async-start | bytes 3145728 | tf_op jit(solution)/shard_map/all_to_all | solution.py:17
  24.6 348.4 %all-reduce.3.cloned.1.call-start = ((), (), s32[]{:S(2)}) async-start(), calls=%async_computation.5 | async-start | bytes 12582912 | tf_op jit(solution)/shard_map/psum | solution.py:9
  67.6 612.2 %all-gather.7.cloned.1.call-start = ((), (), s32[]{:S(2)}) async-start(), calls=%async_computation.2 | async-start | bytes 4259840 | tf_op jit(solution)/shard_map/all_gather | solution.py:20
  68.3 914.4 %all-gather.9.cloned.1.call-start = ((), (), s32[]{:S(2)}) async-start(), calls=%async_computation.3 | async-start | bytes 4259840 | tf_op jit(solution)/shard_map/all_gather | solution.py:20
  69.1 1216.6 %all-gather.11.cloned.1.call-start = ((), (), s32[]{:S(2)}) async-start(), calls=%async_computation.4 | async-start | bytes 4259840 | tf_op jit(solution)/shard_map/all_gather | solution.py:20
  372.9 306.8 %copy-start.2 = (bf16[384,2048]{0,1:T(8,128)(2,1)S(1)}, bf16[384,2048]{0,1:T(8,128)(2,1)}, u32[]{:S(2)}) copy-start(bf16[384,2048]{0,1:T(8,128)(2,1)} %get-tuple-element.6) | copy-start | bytes 4718596
  982.7 302.9 %copy-start = (bf16[384,2048]{0,1:T(8,128)(2,1)S(1)}, bf16[384,2048]{0,1:T(8,128)(2,1)}, u32[]{:S(2)}) copy-start(bf16[384,2048]{0,1:T(8,128)(2,1)} %get-tuple-element.8) | copy-start | bytes 4718596
  982.7 302.9 %copy-start.1 = (f32[384,1024]{1,0:T(8,128)S(1)}, f32[384,1024]{1,0:T(8,128)}, u32[]{:S(2)}) copy-start(f32[384,1024]{1,0:T(8,128)} %param.5) | copy-start | bytes 4718596
Sparse Core Ops, SparseCore 0:
  10.0 362.9 all-gather.4
  374.7 304.9 all-gather.6
  681.5 301.1 all-gather.8
  984.4 301.1 all-gather.10
Sparse Core Ops, SparseCore 1:
  67.7 142.4 all-reduce.2
where the time goes:
time: 1310 us; the launch traced here: 1300 us
  waiting for transfers between devices  1240 us (95%)
  matrix products  23.2 us (2%)
  between operations  14.6 us (1%)
    all_gather x4, waiting for transfers between devices, per_device(): panel_ints = lax.all_gather(stacked[column], 'wide', axis=0, tiled=True)  1200 us
    all_to_all x1, waiting for transfers between devices, per_device(): lax.all_to_all(amplitudes, 'wide', split_axis=0, concat_axis=1, tiled=True)  40.1 us
  transfers between devices with their start and end apart: 6, of which 5 were waited for; matrix products, arithmetic and copies ran while one was open for 2% of the time, Pallas kernels for 0%

commit v1 on v0

v1 whole, which is shorter than its diff:
```python
import jax
import jax.numpy as jnp
from jax import lax
from jax.sharding import Mesh, PartitionSpec as P

AXES = ("z", "x_lo", "y", "x_hi", "core")
SIZES = (8, 2, 4, 2, 2)
SPLIT = 512


def swap(value, axis):
    return lax.ppermute(value, axis, [(0, 1), (1, 0)])


def gather(value, axis):
    return lax.all_gather(value, axis, axis=0)


def per_device(amplitudes, integrals, old_residual):
    x_lo = lax.axis_index("x_lo")
    place = lax.axis_index("x_hi") * 2 + lax.axis_index("core")
    cds = amplitudes.shape[1]
    rows, cols = old_residual.shape
    groups = integrals.reshape(4, cds, cols)
    sets = [lax.dynamic_index_in_dim(groups, place ^ s, 0, keepdims=False) for s in range(4)]
    panel = jnp.stack(sets)
    left, right = panel[..., :SPLIT], panel[..., SPLIT:]
    left = gather(gather(left, "y"), "z")
    right = gather(gather(right, "z"), "y")
    right = right.transpose(1, 0, 2, 3, 4)

    blocks = amplitudes.T.reshape(cds, 8, 2, 4, rows)

    def rows_of(side):
        sent = lax.dynamic_index_in_dim(blocks, side, 2, keepdims=False)
        sent = sent.transpose(1, 2, 0, 3).reshape(32, cds, rows)
        own = lax.all_to_all(sent, ("z", "y"), split_axis=0, concat_axis=0, tiled=True)
        far = swap(own, "x_hi")
        return jnp.stack([own, swap(own, "core"), far, swap(far, "core")], 1).reshape(-1, rows)

    def multiply(amps):
        halves = [
            lax.dot_general(
                amps, b.reshape(-1, b.shape[-1]), (((0,), (0,)), ((), ())),
                preferred_element_type=jnp.float32,
            )
            for b in (left, right)
        ]
        return jnp.concatenate(halves, 1)

    theirs = multiply(rows_of(1 - x_lo))
    received = swap(theirs, "x_lo")
    return old_residual + multiply(rows_of(x_lo)) + received


def solution(mesh):
    fine = Mesh(mesh.devices.reshape(SIZES), AXES)
    wide, narrow = ("z", "x_lo", "y"), ("x_hi", "core")
    placed = (P(None, wide + narrow), P(wide, narrow), P(wide, narrow))
    return jax.shard_map(
        per_device, mesh=fine, in_specs=placed, out_specs=P(wide, narrow), check_vma=False
    )
```

time: 1310 us -> 235 us (0.18)
  waiting for transfers between devices: 1240 us -> 158 us
  blocking collectives: 0 us -> 14.2 us
    all_gather x4 -> x3, waiting for transfers between devices: 1200 us -> 70.4 us  [gather(): return lax.all_gather(value, axis, axis=0)]
    ppermute x0 -> x7, waiting for transfers between devices: none -> 38.5 us  [swap(): return lax.ppermute(value, axis, [(0, 1), (1, 0)])]
    all_gather x0 -> x1, blocking collectives: none -> 14.2 us  [gather(): return lax.all_gather(value, axis, axis=0)]
    all_to_all x1 -> x2, waiting for transfers between devices: 40.1 us -> 48.8 us  [rows_of(): lax.all_to_all(sent, ('z', 'y'), split_axis=0, concat_axis=0, tiled=True)]
  transfers between devices with their start and end apart: 6 -> 12, of which waited for: 5 -> 6; matrix products, arithmetic and copies ran while one was open for 2% -> 9% of each run, Pallas kernels for 0% -> 0%
where the time goes in v1:
time: 235 us; the launch traced here: 232 us
  waiting for transfers between devices  158 us (67%)
  starting transfers between devices  20.5 us (9%)
  blocking collectives  14.2 us (6%)
  between operations  13.2 us (6%)
  matrix products  10.4 us (4%)
  local copies, waits for them, and re-layouts  9.83 us (4%)
  other arithmetic  6.35 us (3%)
    all_gather x3, waiting for transfers between devices, gather(): return lax.all_gather(value, axis, axis=0)  70.4 us
    all_to_all x2, waiting for transfers between devices, rows_of(): lax.all_to_all(sent, ('z', 'y'), split_axis=0, concat_axis=0, tiled=True)  48.8 us
    ppermute x7, waiting for transfers between devices, swap(): return lax.ppermute(value, axis, [(0, 1), (1, 0)])  38.5 us
    all_gather x1, blocking collectives, gather(): return lax.all_gather(value, axis, axis=0)  14.2 us
    all_to_all x2, starting transfers between devices, rows_of(): lax.all_to_all(sent, ('z', 'y'), split_axis=0, concat_axis=0, tiled=True)  12 us
    dot_general x4, matrix products, multiply(): lax.dot_general(amps, b.reshape(-1, b.shape[-1]), (((0,), (0,)), ((), ())...  10.4 us
    ppermute x7, starting transfers between devices, swap(): return lax.ppermute(value, axis, [(0, 1), (1, 0)])  8.39 us
  transfers between devices with their start and end apart: 12, of which 6 were waited for; matrix products, arithmetic and copies ran while one was open for 9% of the time, Pallas kernels for 0%

profile of v1, /device:TPU:24, one launch (start us, length us, event | category | flops | bytes accessed | tf_op | source)
XLA Modules:
  0.0 232.3 jit_solution(11729277428098931547)
XLA Ops:
  6.5 1.1 constant_dynamic-slice_fusion.4
  8.4 14.2 %all-gather = bf16[16,32,512]{2,1,0:T(8,128)(2,1)} all-gather(bf16[4,32,512]{2,1,0:T(8,128)(2,1)S(1)} %get-tuple-element.7), channel_id=2, replica_groups=mesh['z'=8,'x_lo'=2,'y'=4,'x_hi'=2,'core'=2] {'y'}, dimensions={0}, use_global_device_ids=true | all-gather | bytes 655360 | tf_op jit(solution)/shard_map/all_gather | solution.py:16
  22.7 27.9 %all-gather.10.cloned.1.call-done = bf16[32,32,512]{2,1,0:T(8,128)(2,1)} async-done(((bf16[4,32,512]{2,1,0:T(8,128)(2,1)}), bf16[32,32,512]{2,1,0:T(8,128)(2,1)}) %all-gather.10.cloned.1.call-update) | async-done | bytes 1048592 | tf_op jit(solution)/shard_map/all_gather | solution.py:16
  50.6 1.2 reshape.26
  52.5 1.1 copy.26
  53.6 7.1 %all-to-all-start.1 = ((bf16[32,32,384]{2,1,0:T(8,128)(2,1)}), bf16[32,32,384]{2,1,0:T(8,128)(2,1)S(1)}, u32[]{:S(2)}, u32[]{:S(2)}) async-start(bf16[32,32,384]{2,1,0:T(8,128)(2,1)} %bitcast.21), calls=%async_computation.1 | async-start | bytes 1572864 | tf_op jit(solution)/shard_map/all_to_all | solution.py:37
  60.7 1.2 copy.21
  62.0 25.4 %all-to-all-done.1 = bf16[32,32,384]{2,1,0:T(8,128)(2,1)S(1)} async-done(((bf16[32,32,384]{2,1,0:T(8,128)(2,1)}), bf16[32,32,384]{2,1,0:T(8,128)(2,1)S(1)}, u32[]{:S(2)}, u32[]{:S(2)}) %all-to-all-start.1) | async-done | bytes 786464 | tf_op jit(solution)/shard_map/all_to_all | solution.py:37
  87.4 4.9 %all-to-all-start = ((bf16[32,32,384]{2,1,0:T(8,128)(2,1)}), bf16[32,32,384]{2,1,0:T(8,128)(2,1)S(1)}, u32[]{:S(2)}, u32[]{:S(2)}) async-start(bf16[32,32,384]{2,1,0:T(8,128)(2,1)} %bitcast.3), calls=%async_computation | async-start | bytes 1572864 | tf_op jit(solution)/shard_map/all_to_all | solution.py:37
  92.3 3.1 %collective-permute-start.4 = (bf16[32,32,384]{2,1,0:T(8,128)(2,1)S(1)}, bf16[32,32,384]{2,1,0:T(8,128)(2,1)}, u32[]{:S(2)}, u32[]{:S(2)}) collective-permute-start(bf16[32,32,384]{2,1,0:T(8,128)(2,1)S(1)} %all-to-all-done.1), channel_id=1, source_target_pairs={{0,2},{2,0},{1,3},{3,1},{4,6},{6,4},{5,7},{7,5},{8,10},{10,8},{9,1... | collective-permute-start | bytes 2359304 | tf_op jit(solution)/shard_map/ppermute | solution.py:12
  95.4 23.4 %all-to-all-done = bf16[32,32,384]{2,1,0:T(8,128)(2,1)S(1)} async-done(((bf16[32,32,384]{2,1,0:T(8,128)(2,1)}), bf16[32,32,384]{2,1,0:T(8,128)(2,1)S(1)}, u32[]{:S(2)}, u32[]{:S(2)}) %all-to-all-start) | async-done | bytes 786464 | tf_op jit(solution)/shard_map/all_to_all | solution.py:37
  118.8 2.8 %collective-permute-start.1 = (bf16[32,32,384]{2,1,0:T(8,128)(2,1)S(1)}, bf16[32,32,384]{2,1,0:T(8,128)(2,1)S(1)}, u32[]{:S(2)}, u32[]{:S(2)}) collective-permute-start(bf16[32,32,384]{2,1,0:T(8,128)(2,1)S(1)} %all-to-all-done), channel_id=1, source_target_pairs={{0,2},{2,0},{1,3},{3,1},{4,6},{6,4},{5,7},{7,5},{8,10},{10,8},{9,1... | collective-permute-start | bytes 2359304 | tf_op jit(solution)/shard_map/ppermute | solution.py:12
  122.1 10.2 %collective-permute-done.1 = bf16[32,32,384]{2,1,0:T(8,128)(2,1)S(1)} collective-permute-done((bf16[32,32,384]{2,1,0:T(8,128)(2,1)S(1)}, bf16[32,32,384]{2,1,0:T(8,128)(2,1)S(1)}, u32[]{:S(2)}, u32[]{:S(2)}) %collective-permute-start.1) | collective-permute-done | bytes 786464 | tf_op jit(solution)/shard_map/ppermute | solution.py:12
  132.3 2.9 %pad_maximum_fusion.1 = bf16[32,4,32,384]{3,2,1,0:T(8,128)(2,1)} fusion(bf16[32,1,32,384]{3,2,1,0:T(8,128)(2,1)S(1)} %bitcast.64, bf16[32,1,32,384]{3,2,1,0:T(8,128)(2,1)} %bitcast.27, bf16[32,1,32,384]{3,2,1,0:T(8,128)(2,1)S(1)} %bitcast.63, bf16[32,1,32,384]{3,2,1,0:T(8,128)(2,1)S(1)} %bitcast.53), kind=kLoop, calls=%fused_computation.1 | loop fusion | flops 4718592 | bytes 6291456 | tf_op jit(solution)/shard_map/stack | solution.py:39
  135.2 5.0 %fusion.4 = f32[384,512]{1,0:T(8,128)S(1)} fusion(bf16[4096,384]{1,0:T(8,128)(2,1)} %bitcast.54, bf16[4096,512]{1,0:T(8,128)(2,1)} %bitcast.66), kind=kOutput, calls=%fused_computation.15 | convolution fusion | flops 1610612736 | bytes 8126464 | tf_op jit(solution)/shard_map/dot_general | solution.py:43
  140.2 42.5 %all-gather.12.cloned.1.call-done = bf16[32,4,32,512]{3,2,1,0:T(8,128)(2,1)} async-done(((bf16[8,4,32,512]{3,2,1,0:T(8,128)(2,1)}), bf16[32,4,32,512]{3,2,1,0:T(8,128)(2,1)}) %all-gather.12.cloned.1.call-update) | async-done | bytes 4194320 | tf_op jit(solution)/shard_map/all_gather | solution.py:16
  182.7 2.8 %copy.25 = bf16[8,4,4,32,512]{4,3,2,1,0:T(8,128)(2,1)S(1)} copy(bf16[8,4,4,32,512]{4,3,2,0,1:T(8,128)(2,1)} %bitcast.49) | data formatting | bytes 8388608 | tf_op jit(solution)/shard_map/transpose | solution.py:30
  185.8 1.8 fusion.5
  187.8 2.0 collective-permute-start.6
  189.8 1.7 pad_maximum_fusion
  192.2 1.8 fusion.2
  194.0 1.8 fusion.3
  195.8 28.3 %collective-permute-done.6 = f32[384,1024]{1,0:T(8,128)S(1)} collective-permute-done((f32[384,1024]{1,0:T(8,128)S(1)}, f32[384,1024]{1,0:T(8,128)S(1)}, u32[]{:S(2)}, u32[]{:S(2)}) %collective-permute-start.6) | collective-permute-done | bytes 1572896 | tf_op jit(solution)/shard_map/ppermute | solution.py:12
  224.2 1.6 fusion
  (28 shorter events, 3.2 us)
Async XLA Ops:
  6.5 44.1 %copy-start.1 = (bf16[24576,32]{0,1:T(8,128)(2,1)S(1)}, bf16[24576,32]{0,1:T(8,128)(2,1)}, u32[]{:S(2)}) copy-start(bf16[24576,32]{0,1:T(8,128)(2,1)} %param.3) | copy-start | bytes 4718596
  6.5 44.1 %all-gather.10.cloned.1.call-start = ((), (), s32[]{:S(2)}) async-start(), calls=%async_computation.3 | async-start | bytes 1179648 | tf_op jit(solution)/shard_map/all_gather | solution.py:16
  8.4 126.9 %all-gather.8.cloned.1.call-start = ((), (), s32[]{:S(2)}) async-start(), calls=%async_computation.2 | async-start | bytes 4718592 | tf_op jit(solution)/shard_map/all_gather | solution.py:16
  22.6 160.1 %all-gather.12.cloned.1.call-start = ((), (), s32[]{:S(2)}) async-start(), calls=%async_computation.4 | async-start | bytes 5242880 | tf_op jit(solution)/shard_map/all_gather | solution.py:16
  53.6 33.8 %all-to-all-start.1 = ((bf16[32,32,384]{2,1,0:T(8,128)(2,1)}), bf16[32,32,384]{2,1,0:T(8,128)(2,1)S(1)}, u32[]{:S(2)}, u32[]{:S(2)}) async-start(bf16[32,32,384]{2,1,0:T(8,128)(2,1)} %bitcast.21), calls=%async_computation.1 | async-start | bytes 1572864 | tf_op jit(solution)/shard_map/all_to_all | solution.py:37
  87.4 31.4 %all-to-all-start = ((bf16[32,32,384]{2,1,0:T(8,128)(2,1)}), bf16[32,32,384]{2,1,0:T(8,128)(2,1)S(1)}, u32[]{:S(2)}, u32[]{:S(2)}) async-start(bf16[32,32,384]{2,1,0:T(8,128)(2,1)} %bitcast.3), calls=%async_computation | async-start | bytes 1572864 | tf_op jit(solution)/shard_map/all_to_all | solution.py:37
  92.3 29.3 %collective-permute-start.4 = (bf16[32,32,384]{2,1,0:T(8,128)(2,1)S(1)}, bf16[32,32,384]{2,1,0:T(8,128)(2,1)}, u32[]{:S(2)}, u32[]{:S(2)}) collective-permute-start(bf16[32,32,384]{2,1,0:T(8,128)(2,1)S(1)} %all-to-all-done.1), channel_id=1, source_target_pairs={{0,2},{2,0},{1,3},{3,1},{4,6},{6,4},{5,7},{7,5},{8,10},{10,8},{9,1... | collective-permute-start | bytes 2359304 | tf_op jit(solution)/shard_map/ppermute | solution.py:12
  118.8 13.5 %collective-permute-start.1 = (bf16[32,32,384]{2,1,0:T(8,128)(2,1)S(1)}, bf16[32,32,384]{2,1,0:T(8,128)(2,1)S(1)}, u32[]{:S(2)}, u32[]{:S(2)}) collective-permute-start(bf16[32,32,384]{2,1,0:T(8,128)(2,1)S(1)} %all-to-all-done), channel_id=1, source_target_pairs={{0,2},{2,0},{1,3},{3,1},{4,6},{6,4},{5,7},{7,5},{8,10},{10,8},{9,1... | collective-permute-start | bytes 2359304 | tf_op jit(solution)/shard_map/ppermute | solution.py:12
  121.6 10.7 %collective-permute-start.3 = (bf16[32,32,384]{2,1,0:T(8,128)(2,1)S(1)}, bf16[32,32,384]{2,1,0:T(8,128)(2,1)S(1)}, u32[]{:S(2)}, u32[]{:S(2)}) collective-permute-start(bf16[32,32,384]{2,1,0:T(8,128)(2,1)S(1)} %all-to-all-done.1), channel_id=1, source_target_pairs={{0,1},{1,0},{2,3},{3,2},{4,5},{5,4},{6,7},{7,6},{8,9},{9,8},{10,11... | collective-permute-start | bytes 2359304 | tf_op jit(solution)/shard_map/ppermute | solution.py:12
  121.6 10.7 %collective-permute-start.5 = (bf16[32,32,384]{2,1,0:T(8,128)(2,1)}, bf16[32,32,384]{2,1,0:T(8,128)(2,1)S(1)}, u32[]{:S(2)}, u32[]{:S(2)}) collective-permute-start(bf16[32,32,384]{2,1,0:T(8,128)(2,1)} %collective-permute-done.4), channel_id=1, source_target_pairs={{0,1},{1,0},{2,3},{3,2},{4,5},{5,4},{6,7},{7,6},{8,9},{9,8},{10,11... | collective-permute-start | bytes 2359304 | tf_op jit(solution)/shard_map/ppermute | solution.py:12
  122.1 67.6 %collective-permute-start = (bf16[32,32,384]{2,1,0:T(8,128)(2,1)S(1)}, bf16[32,32,384]{2,1,0:T(8,128)(2,1)S(1)}, u32[]{:S(2)}, u32[]{:S(2)}) collective-permute-start(bf16[32,32,384]{2,1,0:T(8,128)(2,1)S(1)} %all-to-all-done), channel_id=1, source_target_pairs={{0,1},{1,0},{2,3},{3,2},{4,5},{5,4},{6,7},{7,6},{8,9},{9,8},{10,11... | collective-permute-start | bytes 2359304 | tf_op jit(solution)/shard_map/ppermute | solution.py:12
  132.3 57.5 %collective-permute-start.2 = (bf16[32,32,384]{2,1,0:T(8,128)(2,1)S(1)}, bf16[32,32,384]{2,1,0:T(8,128)(2,1)}, u32[]{:S(2)}, u32[]{:S(2)}) collective-permute-start(bf16[32,32,384]{2,1,0:T(8,128)(2,1)S(1)} %collective-permute-done.1), channel_id=1, source_target_pairs={{0,1},{1,0},{2,3},{3,2},{4,5},{5,4},{6,7},{7,6},{8,9},{9,8},{10,11... | collective-permute-start | bytes 2359304 | tf_op jit(solution)/shard_map/ppermute | solution.py:12
  182.7 3.2 %copy-start = (bf16[32,4,32,384]{3,2,1,0:T(8,128)(2,1)S(1)}, bf16[32,4,32,384]{3,2,1,0:T(8,128)(2,1)}, u32[]{:S(2)}) copy-start(bf16[32,4,32,384]{3,2,1,0:T(8,128)(2,1)} %pad_maximum_fusion.1) | copy-start | bytes 9437188
  187.8 36.4 %collective-permute-start.6 = (f32[384,1024]{1,0:T(8,128)S(1)}, f32[384,1024]{1,0:T(8,128)S(1)}, u32[]{:S(2)}, u32[]{:S(2)}) collective-permute-start(f32[384,1024]{1,0:T(8,128)S(1)} %pad_maximum_fusion.2), channel_id=1, source_target_pairs={{0,16},{16,0},{1,17},{17,1},{2,18},{18,2},{3,19},{19,3},{4,20},{20... | collective-permute-start | bytes 4718600 | tf_op jit(solution)/shard_map/ppermute | solution.py:12
  189.8 2.4 %copy-start.3 = (bf16[32,4,32,512]{3,2,1,0:T(8,128)(2,1)S(1)}, bf16[32,4,32,512]{3,2,1,0:T(8,128)(2,1)}, u32[]{:S(2)}) copy-start(bf16[32,4,32,512]{3,2,1,0:T(8,128)(2,1)} %all-gather.8.cloned.1.call-done) | copy-start | bytes 12582916
  194.0 30.2 %copy-start.2 = (f32[384,1024]{1,0:T(8,128)S(1)}, f32[384,1024]{1,0:T(8,128)}, u32[]{:S(2)}) copy-start(f32[384,1024]{1,0:T(8,128)} %param.5) | copy-start | bytes 4718596
Sparse Core Ops, SparseCore 0:
  9.1 41.4 all-gather.9
  52.4 80.7 all-gather.7
  135.0 47.6 all-gather.11

commit v2 on v0

v2 whole, which is shorter than its diff:
```python
import jax
import jax.numpy as jnp
from jax import lax
from jax.experimental import pallas as pl
from jax.experimental.pallas import tpu as pltpu
from jax.sharding import Mesh, PartitionSpec as P

AXES = ("z", "x_lo", "y", "x_hi", "core")
SIZES = (8, 2, 4, 2, 2)
NZ, NY, NS = 8, 4, 2
NEAR, FAR = (0, 1, 7, 2), (6, 3, 5, 4)
PANELS = (512, 512)
SENT = jnp.float16


def shift(value, axis, by):
    size = SIZES[AXES.index(axis)]
    return lax.ppermute(value, axis, [(i, (i + by) % size) for i in range(size)])


def across(value):
    return lax.ppermute(value, ("x_lo", "x_hi"), [(i, 3 - i) for i in range(4)])


def tie(*values):
    return lax.optimization_barrier(values)


def call(kernel, out_shape, args, place=None):
    vmem = pl.BlockSpec(memory_space=pltpu.VMEM)
    smem = pl.BlockSpec(memory_space=pltpu.SMEM)
    first = [] if place is None else [place]
    many = isinstance(out_shape, list)
    return pl.pallas_call(
        kernel,
        out_shape=out_shape,
        in_specs=[smem] * len(first) + [vmem] * len(args),
        out_specs=[vmem] * len(out_shape) if many else vmem,
        compiler_params=pltpu.CompilerParams(vmem_limit_bytes=16 * 2**20),
        cost_estimate=pl.CostEstimate(flops=1, bytes_accessed=1, transcendentals=0),
    )(*first, *args)


def cut_kernel(place, amps, out):
    rows = out.shape[-1] // 2
    for y in range(NY):
        for z in range(NZ):
            for side in range(2):
                at = (z * 2 + lax.rem(place[0] + 1 + side, 2)) * NY + y
                cols = pl.ds(pl.multiple_of(at * rows, 128), rows)
                out[y, z, :, side * rows : (side + 1) * rows] = amps[:, cols]


def pack_kernel(amps, out):
    for y in range(NY):
        for z in range(NZ):
            out[z, y] = amps[y, z]


def turn_kernel(place, amps, theirs, mine):
    rows = theirs.shape[0]
    for dz in range(NZ):
        from_z = lax.rem(place[0] - dz + NZ, NZ)
        block = [amps[from_z, lax.rem(place[1] - dy + NY, NY)] for dy in range(NY)]
        block = jnp.concatenate(block, 0)
        width = block.shape[0]
        theirs[:, dz * width : (dz + 1) * width] = block[:, :rows].T
        mine[:, dz * width : (dz + 1) * width] = block[:, rows:].T


def stack_kernel(col, *refs):
    *blocks, out = refs
    for i, block in enumerate(blocks):
        out[i] = block[:, :, col : col + out.shape[-1]]


def stack(blocks, col, width):
    sets, cds, _ = blocks[0].shape
    shape = jax.ShapeDtypeStruct((len(blocks), sets, cds, width), blocks[0].dtype)
    return call(lambda *refs: stack_kernel(col, *refs), shape, blocks)


def multiply(amps, near, far, col, width):
    rows = amps[0].shape[0]
    deep = amps[0].shape[1] // 2

    def kernel(a0, a1, *refs):
        near_refs, far_refs, outs = refs[:5], refs[5:9], refs[9:]

        def block_of(dz, dy, entry, at, size):
            if dz in FAR:
                return far_refs[dy][FAR.index(dz), entry, :, at : at + size]
            z, cols = NEAR.index(dz), slice(col + at, col + at + size)
            if dy == 2:
                half = len(NEAR) // 2
                return near_refs[2 + z // half][z % half, entry, :, cols]
            return near_refs[{0: 0, 1: 1, 3: 4}[dy]][z, entry, :, cols]

        for h, out in enumerate(outs):
            for at in range(0, width, 256):
                total = None
                for part in range(2):
                    block = jnp.concatenate(
                        [
                            block_of(part * 4 + dz, dy, h * NS + s, at, 256)
                            for s in range(NS)
                            for dz in range(4)
                            for dy in range(NY)
                        ],
                        0,
                    )
                    lhs = jnp.concatenate(
                        [a[:, part * deep : (part + 1) * deep] for a in (a0, a1)], 1
                    )
                    term = jnp.dot(lhs, block, preferred_element_type=jnp.float32)
                    total = term if total is None else total + term
                out[:, at : at + 256] = total

    shape = jax.ShapeDtypeStruct((rows, width), jnp.float32)
    return call(kernel, [shape, shape], [*amps, *near, *far])


def along_y(value):
    return shift(value, "y", 1), shift(value, "y", -1)


def beyond(up, down):
    half = up.shape[0] // 2
    return shift(up[:half], "y", 1), shift(down[half:], "y", -1)


def per_device(amplitudes, integrals, old_residual):
    z, x_lo, y, x_hi, core = (lax.axis_index(a) for a in AXES)
    cds = amplitudes.shape[1]
    rows, cols = old_residual.shape
    groups = integrals.reshape(2 * NS, cds, cols)

    def group(of_x, s):
        return lax.dynamic_index_in_dim(groups, of_x * NS + (core ^ s), 0, keepdims=True)

    away = jnp.concatenate([group(1 - x_hi, s) for s in range(NS)])
    here = [group(x_hi, s) for s in range(NS)]
    ints = jnp.concatenate(here + [shift(away, "x_hi", 1)])

    kind = amplitudes.dtype
    shape = jax.ShapeDtypeStruct((NY, NZ, cds, 2 * rows), kind)
    cut = call(cut_kernel, shape, [amplitudes.T], x_lo.reshape(1).astype(jnp.int32))
    ints, cut = tie(ints, cut)
    got = lax.all_to_all(cut, "y", split_axis=0, concat_axis=0, tiled=True)

    def along_z(amps):
        return lax.all_to_all(amps, "z", split_axis=0, concat_axis=0, tiled=True)

    ring = {0: ints}
    for step in (1, 2):
        ring[step] = shift(ring[step - 1], "z", 1)
        ring[NZ - step] = shift(ring[-(step - 1) % NZ], "z", -1)
    near = stack([ring[d] for d in NEAR], 0, cols)
    near, got, ring[2], ring[6] = tie(near, got, ring[2], ring[6])
    near_up, near_down = along_y(near)
    ring[3], ring[5] = shift(ring[2], "z", 1), shift(ring[6], "z", -1)
    ring[4] = shift(ring[3], "z", 1)
    shape = jax.ShapeDtypeStruct((NZ, NY, cds, 2 * rows), kind)
    packed = call(pack_kernel, shape, [got])
    far_z, packed = tie([ring[d] for d in FAR], packed)
    starts = [sum(PANELS[:i]) for i in range(len(PANELS))]
    own = [stack(far_z, at, width) for at, width in zip(starts, PANELS)]
    packed, own, near_up, near_down = tie(packed, own, near_up, near_down)
    amps = along_z(packed)

    near_two = beyond(near_up, near_down)
    near = [near, near_up, *near_two, near_down]
    far = [[own[0], *[shift(own[0], "y", d) for d in (1, 2, 3)]]]
    far[0][1], far[0][3], own[1] = tie(far[0][1], far[0][3], own[1])
    far.append([own[1], *[shift(own[1], "y", d) for d in (1, 2, 3)]])
    amps, near, far[0][2] = tie(amps, near, far[0][2])
    place = jnp.stack([z, y]).astype(jnp.int32)
    shape = jax.ShapeDtypeStruct((rows, NZ * NY * cds), kind)
    theirs, mine = call(turn_kernel, [shape, shape], [amps], place)
    theirs = [theirs, shift(theirs, "core", 1)]
    mine = [mine, shift(mine, "core", 1)]
    totals, at = [], 0
    for panel, width in zip(far, PANELS):
        first, second = multiply(theirs, near, panel, at, width)
        first = shift(first.astype(SENT), "x_lo", 1)
        second = across(second.astype(SENT))
        own, third = multiply(mine, near, panel, at, width)
        third = shift(third.astype(SENT), "x_hi", 1)
        total = own
        for term in (first, second, third):
            total = total + term.astype(jnp.float32)
        totals.append(total)
        at += width
    return old_residual + jnp.concatenate(totals, 1)


def solution(mesh):
    fine = Mesh(mesh.devices.reshape(SIZES), AXES)
    wide, narrow = ("z", "x_lo", "y"), ("x_hi", "core")
    placed = (P(None, wide + narrow), P(wide, narrow), P(wide, narrow))
    return jax.shard_map(
        per_device, mesh=fine, in_specs=placed, out_specs=P(wide, narrow), check_vma=False
    )
```

time: 1310 us -> 159 us (0.12)
  waiting for transfers between devices: 1240 us -> 79.7 us
  starting transfers between devices: 13 us -> 51.3 us
  matrix products: 23.2 us -> 0 us
  Pallas kernels: 0 us -> 16.4 us
  between operations: 14.6 us -> 0.23 us
    all_gather x4 -> x0, waiting for transfers between devices: 1200 us -> none  [per_device(): panel_ints = lax.all_gather(stacked[column], 'wide', axis=0, tiled=True)]
    ppermute x0 -> x26, waiting for transfers between devices: none -> 72.5 us  [the longest x24 62.4 us: shift(): lax.ppermute(value, axis, [(i, (i + by) % size) for i in range(size)])]
    ppermute x0 -> x26, starting transfers between devices: none -> 37 us  [the longest x24 32.7 us: shift(): lax.ppermute(value, axis, [(i, (i + by) % size) for i in range(size)])]
    all_to_all x1 -> x2, waiting for transfers between devices: 40.1 us -> 7.18 us  [the longest x1 7.18 us: along_z(): return lax.all_to_all(amps, 'z', split_axis=0, concat_axis=0, tiled=True)]
    dot_general x4 -> x0, matrix products: 23.2 us -> none  [per_device(): jnp.dot(panel, panel_ints, preferred_element_type=jnp.float32)]
    pallas_call x0 -> x10, Pallas kernels: none -> 16.4 us  [call(): pl.pallas_call(kernel, out_shape=out_shape, in_specs=[smem] * len(first)...]
  transfers between devices with their start and end apart: 6 -> 28, of which waited for: 5 -> 14; matrix products, arithmetic and copies ran while one was open for 2% -> 1% of each run, Pallas kernels for 0% -> 10%
where the time goes in v2:
time: 159 us
  waiting for transfers between devices  79.7 us (50%)
  starting transfers between devices  51.3 us (32%)
  Pallas kernels  16.4 us (10%)
  local copies, waits for them, and re-layouts  9.19 us (6%)
  other arithmetic  2.24 us (1%)
    ppermute x24, waiting for transfers between devices, shift(): lax.ppermute(value, axis, [(i, (i + by) % size) for i in range(size)])  62.4 us
    ppermute x24, starting transfers between devices, shift(): lax.ppermute(value, axis, [(i, (i + by) % size) for i in range(size)])  32.7 us
    pallas_call x10, Pallas kernels, call(): pl.pallas_call(kernel, out_shape=out_shape, in_specs=[smem] * len(first)...  16.4 us
    ppermute x2, waiting for transfers between devices, across(): return lax.ppermute(value, ('x_lo', 'x_hi'), [(i, 3 - i) for i in range(4)])  10.1 us
    all_to_all x1, starting transfers between devices, along_z(): return lax.all_to_all(amps, 'z', split_axis=0, concat_axis=0, tiled=True)  9 us
    all_to_all x1, waiting for transfers between devices, along_z(): return lax.all_to_all(amps, 'z', split_axis=0, concat_axis=0, tiled=True)  7.18 us
    unnamed x18, local copies, waits for them, and re-layouts  6.54 us
    all_to_all x1, starting transfers between devices, per_device(): got = lax.all_to_all(cut, 'y', split_axis=0, concat_axis=0, tiled=True)  5.24 us
  transfers between devices with their start and end apart: 28, of which 14 were waited for; matrix products, arithmetic and copies ran while one was open for 1% of the time, Pallas kernels for 10%

profile of v2, /device:TPU:24, one launch (start us, length us, event | category | flops | bytes accessed | tf_op | source)
XLA Modules:
  0.0 159.0 jit_solution(5602650438046823921)
XLA Ops:
  1.0 3.1 %collective-permute-start = (bf16[2,32,1024]{2,1,0:T(8,128)(2,1)S(1)}, bf16[2,32,1024]{2,1,0:T(8,128)(2,1)S(1)}, u32[]{:S(2)}, u32[]{:S(2)}) collective-permute-start(bf16[2,32,1024]{2,1,0:T(8,128)(2,1)S(1)} %pad_maximum_fusion.1), channel_id=1, source_target_pairs={{0,2},{2,0},{1,3},{3,1},{4,6},{6,4},{5,7},{7,5},{8,10},{10,8},{9,1... | collective-permute-start | bytes 393224 | tf_op jit(solution)/shard_map/ppermute | solution.py:18
  7.8 5.2 %all-to-all-start = ((bf16[4,8,32,768]{3,2,1,0:T(8,128)(2,1)}), bf16[4,8,32,768]{3,2,1,0:T(8,128)(2,1)S(1)}, u32[]{:S(2)}, u32[]{:S(2)}) async-start(bf16[4,8,32,768]{3,2,1,0:T(8,128)(2,1)} %copy-done.3), calls=%async_computation | async-start | bytes 3145728 | tf_op jit(solution)/shard_map/all_to_all | solution.py:149
  14.5 3.9 %collective-permute-start.2 = (bf16[4,32,1024]{2,1,0:T(8,128)(2,1)S(1)}, bf16[4,32,1024]{2,1,0:T(8,128)(2,1)S(1)}, u32[]{:S(2)}, u32[]{:S(2)}) collective-permute-start(bf16[4,32,1024]{2,1,0:T(8,128)(2,1)S(1)} %pad_maximum_fusion.refs_0_), channel_id=1, source_target_pairs={{0,224},{32,0},{64,32},{96,64},{128,96},{160,128},{192,160},{224,1... | collective-permute-start | bytes 786440 | tf_op jit(solution)/shard_map/ppermute | solution.py:18
  18.4 4.9 %collective-permute-done.1.refs_1_ = bf16[4,32,1024]{2,1,0:T(8,128)(2,1)S(1)} collective-permute-done((bf16[4,32,1024]{2,1,0:T(8,128)(2,1)S(1)}, bf16[4,32,1024]{2,1,0:T(8,128)(2,1)S(1)}, u32[]{:S(2)}, u32[]{:S(2)}) %collective-permute-start.1) | collective-permute-done | bytes 262176 | tf_op jit(solution)/shard_map/ppermute | solution.py:18
  23.3 3.2 %collective-permute-start.4 = (bf16[4,32,1024]{2,1,0:T(8,128)(2,1)S(1)}, bf16[4,32,1024]{2,1,0:T(8,128)(2,1)S(1)}, u32[]{:S(2)}, u32[]{:S(2)}) collective-permute-start(bf16[4,32,1024]{2,1,0:T(8,128)(2,1)S(1)} %collective-permute-done.2.refs_2_), channel_id=1, source_target_pairs={{0,224},{32,0},{64,32},{96,64},{128,96},{160,128},{192,160},{224,1... | collective-permute-start | bytes 786440 | tf_op jit(solution)/shard_map/ppermute | solution.py:18
  26.5 4.3 %collective-permute-done.3.refs_3_ = bf16[4,32,1024]{2,1,0:T(8,128)(2,1)S(1)} collective-permute-done((bf16[4,32,1024]{2,1,0:T(8,128)(2,1)S(1)}, bf16[4,32,1024]{2,1,0:T(8,128)(2,1)S(1)}, u32[]{:S(2)}, u32[]{:S(2)}) %collective-permute-start.3) | collective-permute-done | bytes 262176 | tf_op jit(solution)/shard_map/ppermute | solution.py:18
  35.4 3.9 %collective-permute-start.6 = (bf16[4,32,1024]{2,1,0:T(8,128)(2,1)S(1)}, bf16[4,32,1024]{2,1,0:T(8,128)(2,1)S(1)}, u32[]{:S(2)}, u32[]{:S(2)}) collective-permute-start(bf16[4,32,1024]{2,1,0:T(8,128)(2,1)S(1)} %collective-permute-done.4.refs_0_), channel_id=1, source_target_pairs={{0,224},{32,0},{64,32},{96,64},{128,96},{160,128},{192,160},{224,1... | collective-permute-start | bytes 786440 | tf_op jit(solution)/shard_map/ppermute | solution.py:18
  39.4 4.6 %collective-permute-done.5.refs_1_ = bf16[4,32,1024]{2,1,0:T(8,128)(2,1)S(1)} collective-permute-done((bf16[4,32,1024]{2,1,0:T(8,128)(2,1)}, bf16[4,32,1024]{2,1,0:T(8,128)(2,1)S(1)}, u32[]{:S(2)}, u32[]{:S(2)}) %collective-permute-start.5) | collective-permute-done | bytes 262176 | tf_op jit(solution)/shard_map/ppermute | solution.py:18
  45.5 6.0 %collective-permute-done.7.refs_3_ = bf16[4,32,1024]{2,1,0:T(8,128)(2,1)S(1)} collective-permute-done((bf16[4,32,1024]{2,1,0:T(8,128)(2,1)S(1)}, bf16[4,32,1024]{2,1,0:T(8,128)(2,1)S(1)}, u32[]{:S(2)}, u32[]{:S(2)}) %collective-permute-start.7) | collective-permute-done | bytes 262176 | tf_op jit(solution)/shard_map/ppermute | solution.py:18
  56.7 9.0 %all-to-all-start.1 = ((bf16[8,4,32,768]{3,2,1,0:T(8,128)(2,1)}), bf16[8,4,32,768]{3,2,1,0:T(8,128)(2,1)}, u32[]{:S(2)}, u32[]{:S(2)}) async-start(bf16[8,4,32,768]{3,2,1,0:T(8,128)(2,1)} %copy-done), calls=%async_computation.1 | async-start | bytes 3145728 | tf_op jit(solution)/shard_map/all_to_all | solution.py:152
  69.5 2.7 %collective-permute-start.14 = (bf16[4,4,32,512]{3,2,1,0:T(8,128)(2,1)}, bf16[4,4,32,512]{3,2,1,0:T(8,128)(2,1)}, u32[]{:S(2)}, u32[]{:S(2)}) collective-permute-start(bf16[4,4,32,512]{3,2,1,0:T(8,128)(2,1)} %shard_map.40.refs_5_), channel_id=1, source_target_pairs={{0,4},{4,8},{8,12},{12,0},{1,5},{5,9},{9,13},{13,1},{2,6},{6,10},{... | collective-permute-start | bytes 1572872 | tf_op jit(solution)/shard_map/ppermute | solution.py:18
  72.2 16.9 %collective-permute-done.10.refs_2_ = bf16[2,4,32,1024]{3,2,1,0:T(8,128)(2,1)} collective-permute-done((bf16[2,4,32,1024]{3,2,1,0:T(8,128)(2,1)}, bf16[2,4,32,1024]{3,2,1,0:T(8,128)(2,1)}, u32[]{:S(2)}, u32[]{:S(2)}) %collective-permute-start.10) | collective-permute-done | bytes 524320 | tf_op jit(solution)/shard_map/ppermute | solution.py:18
  89.1 6.3 %collective-permute-done.11.refs_3_ = bf16[2,4,32,1024]{3,2,1,0:T(8,128)(2,1)} collective-permute-done((bf16[2,4,32,1024]{3,2,1,0:T(8,128)(2,1)}, bf16[2,4,32,1024]{3,2,1,0:T(8,128)(2,1)}, u32[]{:S(2)}, u32[]{:S(2)}) %collective-permute-start.11) | collective-permute-done | bytes 524320 | tf_op jit(solution)/shard_map/ppermute | solution.py:18
  95.4 7.2 %all-to-all-done.1.amps = bf16[8,4,32,768]{3,2,1,0:T(8,128)(2,1)} async-done(((bf16[8,4,32,768]{3,2,1,0:T(8,128)(2,1)}), bf16[8,4,32,768]{3,2,1,0:T(8,128)(2,1)}, u32[]{:S(2)}, u32[]{:S(2)}) %all-to-all-start.1) | async-done | bytes 1572896 | tf_op jit(solution)/shard_map/all_to_all | solution.py:152
  107.3 3.6 %shard_map.44 = (f32[384,512]{1,0:T(8,128)S(1)}, f32[384,512]{1,0:T(8,128)S(1)}) custom-call(bf16[384,1024]{1,0:T(8,128)(2,1)S(1)} %get-tuple-element.68.a0, bf16[384,1024]{1,0:T(8,128)(2,1)S(1)} %collective-permute-done.16.a1, bf16[4,4,32,1024]{3,2,1,0:T(8,128)(2,1)S(1)} %shard_map.38.refs_0_, bf16[4,4,32,1024]{3,2,1,0:T(8,128)(2,1)S(1)} %collective-permute-done.8.refs_1_, ...), custom_call_target="tpu_custom_call" | custom-call | flops 1 | bytes 1 | tf_op jit(solution)/shard_map/pallas_call | solution.py:34
  112.6 2.2 %collective-permute-start.18 = (f16[384,512]{1,0:T(8,128)(2,1)S(1)}, f16[384,512]{1,0:T(8,128)(2,1)S(1)}, u32[]{:S(2)}, u32[]{:S(2)}) collective-permute-start(f16[384,512]{1,0:T(8,128)(2,1)S(1)} %convert_element_type.38), channel_id=1, source_target_pairs={{0,18},{2,16},{16,2},{18,0},{1,19},{3,17},{17,3},{19,1},{4,22},{6,... | collective-permute-start | bytes 1179656 | tf_op jit(solution)/shard_map/ppermute | solution.py:22
  114.8 3.6 %shard_map.43 = (f32[384,512]{1,0:T(8,128)S(1)}, f32[384,512]{1,0:T(8,128)S(1)}) custom-call(bf16[384,1024]{1,0:T(8,128)(2,1)S(1)} %get-tuple-element.57.a0, bf16[384,1024]{1,0:T(8,128)(2,1)S(1)} %collective-permute-done.13.a1, bf16[4,4,32,1024]{3,2,1,0:T(8,128)(2,1)S(1)} %shard_map.38.refs_0_, bf16[4,4,32,1024]{3,2,1,0:T(8,128)(2,1)S(1)} %collective-permute-done.8.refs_1_, ...), custom_call_target="tpu_custom_call" | custom-call | flops 1 | bytes 1 | tf_op jit(solution)/shard_map/pallas_call | solution.py:34
  120.0 3.0 %collective-permute-start.19 = (f16[384,512]{1,0:T(8,128)(2,1)S(1)}, f16[384,512]{1,0:T(8,128)(2,1)S(1)}, u32[]{:S(2)}, u32[]{:S(2)}) collective-permute-start(f16[384,512]{1,0:T(8,128)(2,1)S(1)} %convert_element_type.40), channel_id=1, source_target_pairs={{0,2},{2,0},{1,3},{3,1},{4,6},{6,4},{5,7},{7,5},{8,10},{10,8},{9,1... | collective-permute-start | bytes 1179656 | tf_op jit(solution)/shard_map/ppermute | solution.py:18
  123.0 9.2 %collective-permute-done.22.refs_8_ = bf16[4,4,32,512]{3,2,1,0:T(8,128)(2,1)S(1)} collective-permute-done((bf16[4,4,32,512]{3,2,1,0:T(8,128)(2,1)S(1)}, bf16[4,4,32,512]{3,2,1,0:T(8,128)(2,1)S(1)}, u32[]{:S(2)}, u32[]{:S(2)}) %collective-permute-start.22) | collective-permute-done | bytes 524320 | tf_op jit(solution)/shard_map/ppermute | solution.py:18
  132.2 3.0 %shard_map.46 = (f32[384,512]{1,0:T(8,128)S(1)}, f32[384,512]{1,0:T(8,128)S(1)}) custom-call(bf16[384,1024]{1,0:T(8,128)(2,1)S(1)} %get-tuple-element.68.a0, bf16[384,1024]{1,0:T(8,128)(2,1)S(1)} %collective-permute-done.16.a1, bf16[4,4,32,1024]{3,2,1,0:T(8,128)(2,1)S(1)} %shard_map.38.refs_0_, bf16[4,4,32,1024]{3,2,1,0:T(8,128)(2,1)S(1)} %collective-permute-done.8.refs_1_, ...), custom_call_target="tpu_custom_call" | custom-call | flops 1 | bytes 1 | tf_op jit(solution)/shard_map/pallas_call | solution.py:34
  136.9 2.2 %collective-permute-start.24 = (f16[384,512]{1,0:T(8,128)(2,1)S(1)}, f16[384,512]{1,0:T(8,128)(2,1)S(1)}, u32[]{:S(2)}, u32[]{:S(2)}) collective-permute-start(f16[384,512]{1,0:T(8,128)(2,1)S(1)} %convert_element_type.44), channel_id=1, source_target_pairs={{0,18},{2,16},{16,2},{18,0},{1,19},{3,17},{17,3},{19,1},{4,22},{6,... | collective-permute-start | bytes 1179656 | tf_op jit(solution)/shard_map/ppermute | solution.py:22
  139.1 3.0 %shard_map.45 = (f32[384,512]{1,0:T(8,128)S(1)}, f32[384,512]{1,0:T(8,128)S(1)}) custom-call(bf16[384,1024]{1,0:T(8,128)(2,1)S(1)} %get-tuple-element.57.a0, bf16[384,1024]{1,0:T(8,128)(2,1)S(1)} %collective-permute-done.13.a1, bf16[4,4,32,1024]{3,2,1,0:T(8,128)(2,1)S(1)} %shard_map.38.refs_0_, bf16[4,4,32,1024]{3,2,1,0:T(8,128)(2,1)S(1)} %collective-permute-done.8.refs_1_, ...), custom_call_target="tpu_custom_call" | custom-call | flops 1 | bytes 1 | tf_op jit(solution)/shard_map/pallas_call | solution.py:34
  143.1 4.2 %collective-permute-done.23 = f16[384,512]{1,0:T(8,128)(2,1)S(1)} collective-permute-done((f16[384,512]{1,0:T(8,128)(2,1)S(1)}, f16[384,512]{1,0:T(8,128)(2,1)S(1)}, u32[]{:S(2)}, u32[]{:S(2)}) %collective-permute-start.23) | collective-permute-done | bytes 393248 | tf_op jit(solution)/shard_map/ppermute | solution.py:18
  147.3 10.1 %collective-permute-done.24 = f16[384,512]{1,0:T(8,128)(2,1)S(1)} collective-permute-done((f16[384,512]{1,0:T(8,128)(2,1)S(1)}, f16[384,512]{1,0:T(8,128)(2,1)S(1)}, u32[]{:S(2)}, u32[]{:S(2)}) %collective-permute-start.24) | collective-permute-done | bytes 393248 | tf_op jit(solution)/shard_map/ppermute | solution.py:22
  (75 shorter events, 33.5 us)
Async XLA Ops:
  7.8 23.7 %all-to-all-start = ((bf16[4,8,32,768]{3,2,1,0:T(8,128)(2,1)}), bf16[4,8,32,768]{3,2,1,0:T(8,128)(2,1)S(1)}, u32[]{:S(2)}, u32[]{:S(2)}) async-start(bf16[4,8,32,768]{3,2,1,0:T(8,128)(2,1)} %copy-done.3), calls=%async_computation | async-start | bytes 3145728 | tf_op jit(solution)/shard_map/all_to_all | solution.py:149
  13.1 10.2 %collective-permute-start.1 = (bf16[4,32,1024]{2,1,0:T(8,128)(2,1)S(1)}, bf16[4,32,1024]{2,1,0:T(8,128)(2,1)S(1)}, u32[]{:S(2)}, u32[]{:S(2)}) collective-permute-start(bf16[4,32,1024]{2,1,0:T(8,128)(2,1)S(1)} %pad_maximum_fusion.refs_0_), channel_id=1, source_target_pairs={{0,32},{32,64},{64,96},{96,128},{128,160},{160,192},{192,224},{224... | collective-permute-start | bytes 786440 | tf_op jit(solution)/shard_map/ppermute | solution.py:18
  14.5 8.8 %collective-permute-start.2 = (bf16[4,32,1024]{2,1,0:T(8,128)(2,1)S(1)}, bf16[4,32,1024]{2,1,0:T(8,128)(2,1)S(1)}, u32[]{:S(2)}, u32[]{:S(2)}) collective-permute-start(bf16[4,32,1024]{2,1,0:T(8,128)(2,1)S(1)} %pad_maximum_fusion.refs_0_), channel_id=1, source_target_pairs={{0,224},{32,0},{64,32},{96,64},{128,96},{160,128},{192,160},{224,1... | collective-permute-start | bytes 786440 | tf_op jit(solution)/shard_map/ppermute | solution.py:18
  23.3 8.3 %collective-permute-start.4 = (bf16[4,32,1024]{2,1,0:T(8,128)(2,1)S(1)}, bf16[4,32,1024]{2,1,0:T(8,128)(2,1)S(1)}, u32[]{:S(2)}, u32[]{:S(2)}) collective-permute-start(bf16[4,32,1024]{2,1,0:T(8,128)(2,1)S(1)} %collective-permute-done.2.refs_2_), channel_id=1, source_target_pairs={{0,224},{32,0},{64,32},{96,64},{128,96},{160,128},{192,160},{224,1... | collective-permute-start | bytes 786440 | tf_op jit(solution)/shard_map/ppermute | solution.py:18
  32.7 22.0 %collective-permute-start.8 = (bf16[4,4,32,1024]{3,2,1,0:T(8,128)(2,1)S(1)}, bf16[4,4,32,1024]{3,2,1,0:T(8,128)(2,1)S(1)}, u32[]{:S(2)}, u32[]{:S(2)}) collective-permute-start(bf16[4,4,32,1024]{3,2,1,0:T(8,128)(2,1)S(1)} %shard_map.38.refs_0_), channel_id=1, source_target_pairs={{0,4},{4,8},{8,12},{12,0},{1,5},{5,9},{9,13},{13,1},{2,6},{6,10},{... | collective-permute-start | bytes 3145736 | tf_op jit(solution)/shard_map/ppermute | solution.py:18
  33.5 23.2 %collective-permute-start.9 = (bf16[4,4,32,1024]{3,2,1,0:T(8,128)(2,1)S(1)}, bf16[4,4,32,1024]{3,2,1,0:T(8,128)(2,1)S(1)}, u32[]{:S(2)}, u32[]{:S(2)}) collective-permute-start(bf16[4,4,32,1024]{3,2,1,0:T(8,128)(2,1)S(1)} %shard_map.38.refs_0_), channel_id=1, source_target_pairs={{0,12},{4,0},{8,4},{12,8},{1,13},{5,1},{9,5},{13,9},{2,14},{6,2},{... | collective-permute-start | bytes 3145736 | tf_op jit(solution)/shard_map/ppermute | solution.py:18
  34.7 9.2 %collective-permute-start.5 = (bf16[4,32,1024]{2,1,0:T(8,128)(2,1)}, bf16[4,32,1024]{2,1,0:T(8,128)(2,1)S(1)}, u32[]{:S(2)}, u32[]{:S(2)}) collective-permute-start(bf16[4,32,1024]{2,1,0:T(8,128)(2,1)} %copy-done.7), channel_id=1, source_target_pairs={{0,32},{32,64},{64,96},{96,128},{128,160},{160,192},{192,224},{224... | collective-permute-start | bytes 786440 | tf_op jit(solution)/shard_map/ppermute | solution.py:18
  35.4 10.0 %collective-permute-start.6 = (bf16[4,32,1024]{2,1,0:T(8,128)(2,1)S(1)}, bf16[4,32,1024]{2,1,0:T(8,128)(2,1)S(1)}, u32[]{:S(2)}, u32[]{:S(2)}) collective-permute-start(bf16[4,32,1024]{2,1,0:T(8,128)(2,1)S(1)} %collective-permute-done.4.refs_0_), channel_id=1, source_target_pairs={{0,224},{32,0},{64,32},{96,64},{128,96},{160,128},{192,160},{224,1... | collective-permute-start | bytes 786440 | tf_op jit(solution)/shard_map/ppermute | solution.py:18
  56.7 45.8 %all-to-all-start.1 = ((bf16[8,4,32,768]{3,2,1,0:T(8,128)(2,1)}), bf16[8,4,32,768]{3,2,1,0:T(8,128)(2,1)}, u32[]{:S(2)}, u32[]{:S(2)}) async-start(bf16[8,4,32,768]{3,2,1,0:T(8,128)(2,1)} %copy-done), calls=%async_computation.1 | async-start | bytes 3145728 | tf_op jit(solution)/shard_map/all_to_all | solution.py:152
  66.6 22.5 %collective-permute-start.10 = (bf16[2,4,32,1024]{3,2,1,0:T(8,128)(2,1)}, bf16[2,4,32,1024]{3,2,1,0:T(8,128)(2,1)}, u32[]{:S(2)}, u32[]{:S(2)}) collective-permute-start(bf16[2,4,32,1024]{3,2,1,0:T(8,128)(2,1)} %slice.6), channel_id=1, source_target_pairs={{0,4},{4,8},{8,12},{12,0},{1,5},{5,9},{9,13},{13,1},{2,6},{6,10},{... | collective-permute-start | bytes 1572872 | tf_op jit(solution)/shard_map/ppermute | solution.py:18
  67.7 27.6 %collective-permute-start.11 = (bf16[2,4,32,1024]{3,2,1,0:T(8,128)(2,1)}, bf16[2,4,32,1024]{3,2,1,0:T(8,128)(2,1)}, u32[]{:S(2)}, u32[]{:S(2)}) collective-permute-start(bf16[2,4,32,1024]{3,2,1,0:T(8,128)(2,1)} %slice.7), channel_id=1, source_target_pairs={{0,12},{4,0},{8,4},{12,8},{1,13},{5,1},{9,5},{13,9},{2,14},{6,2},{... | collective-permute-start | bytes 1572872 | tf_op jit(solution)/shard_map/ppermute | solution.py:18
  69.5 25.9 %collective-permute-start.12 = (bf16[4,4,32,512]{3,2,1,0:T(8,128)(2,1)}, bf16[4,4,32,512]{3,2,1,0:T(8,128)(2,1)}, u32[]{:S(2)}, u32[]{:S(2)}) collective-permute-start(bf16[4,4,32,512]{3,2,1,0:T(8,128)(2,1)} %shard_map.40.refs_5_), channel_id=1, source_target_pairs={{0,8},{4,12},{8,0},{12,4},{1,9},{5,13},{9,1},{13,5},{2,10},{6,14},... | collective-permute-start | bytes 1572872 | tf_op jit(solution)/shard_map/ppermute | solution.py:18
  69.5 35.7 %collective-permute-start.14 = (bf16[4,4,32,512]{3,2,1,0:T(8,128)(2,1)}, bf16[4,4,32,512]{3,2,1,0:T(8,128)(2,1)}, u32[]{:S(2)}, u32[]{:S(2)}) collective-permute-start(bf16[4,4,32,512]{3,2,1,0:T(8,128)(2,1)} %shard_map.40.refs_5_), channel_id=1, source_target_pairs={{0,4},{4,8},{8,12},{12,0},{1,5},{5,9},{9,13},{13,1},{2,6},{6,10},{... | collective-permute-start | bytes 1572872 | tf_op jit(solution)/shard_map/ppermute | solution.py:18
  72.2 33.0 %collective-permute-start.15 = (bf16[4,4,32,512]{3,2,1,0:T(8,128)(2,1)}, bf16[4,4,32,512]{3,2,1,0:T(8,128)(2,1)}, u32[]{:S(2)}, u32[]{:S(2)}) collective-permute-start(bf16[4,4,32,512]{3,2,1,0:T(8,128)(2,1)} %shard_map.40.refs_5_), channel_id=1, source_target_pairs={{0,12},{4,0},{8,4},{12,8},{1,13},{5,1},{9,5},{13,9},{2,14},{6,2},{... | collective-permute-start | bytes 1572872 | tf_op jit(solution)/shard_map/ppermute | solution.py:18
  104.7 7.9 %collective-permute-start.13 = (bf16[384,1024]{1,0:T(8,128)(2,1)S(1)}, bf16[384,1024]{1,0:T(8,128)(2,1)S(1)}, u32[]{:S(2)}, u32[]{:S(2)}) collective-permute-start(bf16[384,1024]{1,0:T(8,128)(2,1)S(1)} %get-tuple-element.57.a0), channel_id=1, source_target_pairs={{0,1},{1,0},{2,3},{3,2},{4,5},{5,4},{6,7},{7,6},{8,9},{9,8},{10,11... | collective-permute-start | bytes 2359304 | tf_op jit(solution)/shard_map/ppermute | solution.py:18
  105.2 14.9 %collective-permute-start.20 = (bf16[4,4,32,512]{3,2,1,0:T(8,128)(2,1)S(1)}, bf16[4,4,32,512]{3,2,1,0:T(8,128)(2,1)S(1)}, u32[]{:S(2)}, u32[]{:S(2)}) collective-permute-start(bf16[4,4,32,512]{3,2,1,0:T(8,128)(2,1)S(1)} %copy-done.5), channel_id=1, source_target_pairs={{0,4},{4,8},{8,12},{12,0},{1,5},{5,9},{9,13},{13,1},{2,6},{6,10},{... | collective-permute-start | bytes 1572872 | tf_op jit(solution)/shard_map/ppermute | solution.py:18
  105.8 17.2 %collective-permute-start.21 = (bf16[4,4,32,512]{3,2,1,0:T(8,128)(2,1)S(1)}, bf16[4,4,32,512]{3,2,1,0:T(8,128)(2,1)S(1)}, u32[]{:S(2)}, u32[]{:S(2)}) collective-permute-start(bf16[4,4,32,512]{3,2,1,0:T(8,128)(2,1)S(1)} %copy-done.5), channel_id=1, source_target_pairs={{0,8},{4,12},{8,0},{12,4},{1,9},{5,13},{9,1},{13,5},{2,10},{6,14},... | collective-permute-start | bytes 1572872 | tf_op jit(solution)/shard_map/ppermute | solution.py:18
  106.7 25.5 %collective-permute-start.22 = (bf16[4,4,32,512]{3,2,1,0:T(8,128)(2,1)S(1)}, bf16[4,4,32,512]{3,2,1,0:T(8,128)(2,1)S(1)}, u32[]{:S(2)}, u32[]{:S(2)}) collective-permute-start(bf16[4,4,32,512]{3,2,1,0:T(8,128)(2,1)S(1)} %copy-done.5), channel_id=1, source_target_pairs={{0,12},{4,0},{8,4},{12,8},{1,13},{5,1},{9,5},{13,9},{2,14},{6,2},{... | collective-permute-start | bytes 1572872 | tf_op jit(solution)/shard_map/ppermute | solution.py:18
  111.0 31.2 %collective-permute-start.17 = (f16[384,512]{1,0:T(8,128)(2,1)S(1)}, f16[384,512]{1,0:T(8,128)(2,1)S(1)}, u32[]{:S(2)}, u32[]{:S(2)}) collective-permute-start(f16[384,512]{1,0:T(8,128)(2,1)S(1)} %convert_element_type.36), channel_id=1, source_target_pairs={{0,16},{16,0},{1,17},{17,1},{2,18},{18,2},{3,19},{19,3},{4,20},{20... | collective-permute-start | bytes 1179656 | tf_op jit(solution)/shard_map/ppermute | solution.py:18
  112.6 30.3 %collective-permute-start.18 = (f16[384,512]{1,0:T(8,128)(2,1)S(1)}, f16[384,512]{1,0:T(8,128)(2,1)S(1)}, u32[]{:S(2)}, u32[]{:S(2)}) collective-permute-start(f16[384,512]{1,0:T(8,128)(2,1)S(1)} %convert_element_type.38), channel_id=1, source_target_pairs={{0,18},{2,16},{16,2},{18,0},{1,19},{3,17},{17,3},{19,1},{4,22},{6,... | collective-permute-start | bytes 1179656 | tf_op jit(solution)/shard_map/ppermute | solution.py:22
  120.0 22.8 %collective-permute-start.19 = (f16[384,512]{1,0:T(8,128)(2,1)S(1)}, f16[384,512]{1,0:T(8,128)(2,1)S(1)}, u32[]{:S(2)}, u32[]{:S(2)}) collective-permute-start(f16[384,512]{1,0:T(8,128)(2,1)S(1)} %convert_element_type.40), channel_id=1, source_target_pairs={{0,2},{2,0},{1,3},{3,1},{4,6},{6,4},{5,7},{7,5},{8,10},{10,8},{9,1... | collective-permute-start | bytes 1179656 | tf_op jit(solution)/shard_map/ppermute | solution.py:18
  135.2 12.1 %collective-permute-start.23 = (f16[384,512]{1,0:T(8,128)(2,1)S(1)}, f16[384,512]{1,0:T(8,128)(2,1)S(1)}, u32[]{:S(2)}, u32[]{:S(2)}) collective-permute-start(f16[384,512]{1,0:T(8,128)(2,1)S(1)} %convert_element_type.42), channel_id=1, source_target_pairs={{0,16},{16,0},{1,17},{17,1},{2,18},{18,2},{3,19},{19,3},{4,20},{20... | collective-permute-start | bytes 1179656 | tf_op jit(solution)/shard_map/ppermute | solution.py:18
  136.9 20.5 %collective-permute-start.24 = (f16[384,512]{1,0:T(8,128)(2,1)S(1)}, f16[384,512]{1,0:T(8,128)(2,1)S(1)}, u32[]{:S(2)}, u32[]{:S(2)}) collective-permute-start(f16[384,512]{1,0:T(8,128)(2,1)S(1)} %convert_element_type.44), channel_id=1, source_target_pairs={{0,18},{2,16},{16,2},{18,0},{1,19},{3,17},{17,3},{19,1},{4,22},{6,... | collective-permute-start | bytes 1179656 | tf_op jit(solution)/shard_map/ppermute | solution.py:22
  142.1 15.2 %collective-permute-start.25 = (f16[384,512]{1,0:T(8,128)(2,1)S(1)}, f16[384,512]{1,0:T(8,128)(2,1)S(1)}, u32[]{:S(2)}, u32[]{:S(2)}) collective-permute-start(f16[384,512]{1,0:T(8,128)(2,1)S(1)} %convert_element_type.46), channel_id=1, source_target_pairs={{0,2},{2,0},{1,3},{3,1},{4,6},{6,4},{5,7},{7,5},{8,10},{10,8},{9,1... | collective-permute-start | bytes 1179656 | tf_op jit(solution)/shard_map/ppermute | solution.py:18
  (13 other events, 56.2 us)

commit v3 on v2

--- a/solution.py
+++ b/solution.py
@@ -85,16 +85,17 @@
     deep = amps[0].shape[1] // 2
 
     def kernel(a0, a1, *refs):
-        near_refs, far_refs, outs = refs[:5], refs[5:9], refs[9:]
+        near_refs, far_refs, outs = refs[:5], refs[5:-2], refs[-2:]
 
         def block_of(dz, dy, entry, at, size):
-            if dz in FAR:
-                return far_refs[dy][FAR.index(dz), entry, :, at : at + size]
-            z, cols = NEAR.index(dz), slice(col + at, col + at + size)
+            group, order, base = (near_refs, NEAR, col) if dz in NEAR else (far_refs, FAR, 0)
+            z, cols = order.index(dz), slice(base + at, base + at + size)
+            if len(group) == NY:
+                return group[dy][z, entry, :, cols]
             if dy == 2:
-                half = len(NEAR) // 2
-                return near_refs[2 + z // half][z % half, entry, :, cols]
-            return near_refs[{0: 0, 1: 1, 3: 4}[dy]][z, entry, :, cols]
+                half = len(order) // 2
+                return group[2 + z // half][z % half, entry, :, cols]
+            return group[{0: 0, 1: 1, 3: 4}[dy]][z, entry, :, cols]
 
         for h, out in enumerate(outs):
             for at in range(0, width, 256):
@@ -172,7 +173,8 @@
     near = [near, near_up, *near_two, near_down]
     far = [[own[0], *[shift(own[0], "y", d) for d in (1, 2, 3)]]]
     far[0][1], far[0][3], own[1] = tie(far[0][1], far[0][3], own[1])
-    far.append([own[1], *[shift(own[1], "y", d) for d in (1, 2, 3)]])
+    ends = along_y(own[1])
+    far.append([own[1], ends[0], *beyond(*ends), ends[1]])
     amps, near, far[0][2] = tie(amps, near, far[0][2])
     place = jnp.stack([z, y]).astype(jnp.int32)
     shape = jax.ShapeDtypeStruct((rows, NZ * NY * cds), kind)

time: 159 us -> 155 us (0.975)
  waiting for transfers between devices: 79.7 us -> 75.1 us
    ppermute x24 -> x25, waiting for transfers between devices: 62.4 us -> 59 us  [shift(): lax.ppermute(value, axis, [(i, (i + by) % size) for i in range(size)])]
    ppermute x24 -> x25, starting transfers between devices: 32.7 us -> 32.6 us  [shift(): lax.ppermute(value, axis, [(i, (i + by) % size) for i in range(size)])]
  transfers between devices with their start and end apart: 28 -> 29, of which waited for: 14 -> 14; matrix products, arithmetic and copies ran while one was open for 1% -> 2% of each run, Pallas kernels for 10% -> 11%
where the time goes in v3:
time: 155 us; the launch traced here: 154 us
  waiting for transfers between devices  75.1 us (48%)
  starting transfers between devices  51.2 us (33%)
  Pallas kernels  16.4 us (11%)
  local copies, waits for them, and re-layouts  9.24 us (6%)
  other arithmetic  2.24 us (1%)
    ppermute x25, waiting for transfers between devices, shift(): lax.ppermute(value, axis, [(i, (i + by) % size) for i in range(size)])  59 us
    ppermute x25, starting transfers between devices, shift(): lax.ppermute(value, axis, [(i, (i + by) % size) for i in range(size)])  32.6 us
    pallas_call x10, Pallas kernels, call(): pl.pallas_call(kernel, out_shape=out_shape, in_specs=[smem] * len(first)...  16.4 us
    all_to_all x1, starting transfers between devices, along_z(): return lax.all_to_all(amps, 'z', split_axis=0, concat_axis=0, tiled=True)  9 us
    ppermute x2, waiting for transfers between devices, across(): return lax.ppermute(value, ('x_lo', 'x_hi'), [(i, 3 - i) for i in range(4)])  8.99 us
    all_to_all x1, waiting for transfers between devices, along_z(): return lax.all_to_all(amps, 'z', split_axis=0, concat_axis=0, tiled=True)  7.18 us
    unnamed x18, local copies, waits for them, and re-layouts  6.55 us
    all_to_all x1, starting transfers between devices, per_device(): got = lax.all_to_all(cut, 'y', split_axis=0, concat_axis=0, tiled=True)  5.24 us
  transfers between devices with their start and end apart: 29, of which 14 were waited for; matrix products, arithmetic and copies ran while one was open for 2% of the time, Pallas kernels for 11%

profile of v3, /device:TPU:24, one launch (start us, length us, event | category | flops | bytes accessed | tf_op | source)
XLA Modules:
  0.0 154.4 jit_solution(2641975871284213422)
XLA Ops:
  1.0 3.1 %collective-permute-start = (bf16[2,32,1024]{2,1,0:T(8,128)(2,1)S(1)}, bf16[2,32,1024]{2,1,0:T(8,128)(2,1)S(1)}, u32[]{:S(2)}, u32[]{:S(2)}) collective-permute-start(bf16[2,32,1024]{2,1,0:T(8,128)(2,1)S(1)} %pad_maximum_fusion.1), channel_id=1, source_target_pairs={{0,2},{2,0},{1,3},{3,1},{4,6},{6,4},{5,7},{7,5},{8,10},{10,8},{9,1... | collective-permute-start | bytes 393224 | tf_op jit(solution)/shard_map/ppermute | solution.py:18
  7.8 5.2 %all-to-all-start = ((bf16[4,8,32,768]{3,2,1,0:T(8,128)(2,1)}), bf16[4,8,32,768]{3,2,1,0:T(8,128)(2,1)S(1)}, u32[]{:S(2)}, u32[]{:S(2)}) async-start(bf16[4,8,32,768]{3,2,1,0:T(8,128)(2,1)} %copy-done.3), calls=%async_computation | async-start | bytes 3145728 | tf_op jit(solution)/shard_map/all_to_all | solution.py:150
  14.5 3.9 %collective-permute-start.2 = (bf16[4,32,1024]{2,1,0:T(8,128)(2,1)S(1)}, bf16[4,32,1024]{2,1,0:T(8,128)(2,1)S(1)}, u32[]{:S(2)}, u32[]{:S(2)}) collective-permute-start(bf16[4,32,1024]{2,1,0:T(8,128)(2,1)S(1)} %pad_maximum_fusion.refs_0_), channel_id=1, source_target_pairs={{0,224},{32,0},{64,32},{96,64},{128,96},{160,128},{192,160},{224,1... | collective-permute-start | bytes 786440 | tf_op jit(solution)/shard_map/ppermute | solution.py:18
  18.4 4.9 %collective-permute-done.1.refs_1_ = bf16[4,32,1024]{2,1,0:T(8,128)(2,1)S(1)} collective-permute-done((bf16[4,32,1024]{2,1,0:T(8,128)(2,1)S(1)}, bf16[4,32,1024]{2,1,0:T(8,128)(2,1)S(1)}, u32[]{:S(2)}, u32[]{:S(2)}) %collective-permute-start.1) | collective-permute-done | bytes 262176 | tf_op jit(solution)/shard_map/ppermute | solution.py:18
  23.3 3.2 %collective-permute-start.4 = (bf16[4,32,1024]{2,1,0:T(8,128)(2,1)S(1)}, bf16[4,32,1024]{2,1,0:T(8,128)(2,1)S(1)}, u32[]{:S(2)}, u32[]{:S(2)}) collective-permute-start(bf16[4,32,1024]{2,1,0:T(8,128)(2,1)S(1)} %collective-permute-done.2.refs_2_), channel_id=1, source_target_pairs={{0,224},{32,0},{64,32},{96,64},{128,96},{160,128},{192,160},{224,1... | collective-permute-start | bytes 786440 | tf_op jit(solution)/shard_map/ppermute | solution.py:18
  26.5 4.3 %collective-permute-done.3.refs_3_ = bf16[4,32,1024]{2,1,0:T(8,128)(2,1)S(1)} collective-permute-done((bf16[4,32,1024]{2,1,0:T(8,128)(2,1)S(1)}, bf16[4,32,1024]{2,1,0:T(8,128)(2,1)S(1)}, u32[]{:S(2)}, u32[]{:S(2)}) %collective-permute-start.3) | collective-permute-done | bytes 262176 | tf_op jit(solution)/shard_map/ppermute | solution.py:18
  35.4 3.9 %collective-permute-start.6 = (bf16[4,32,1024]{2,1,0:T(8,128)(2,1)S(1)}, bf16[4,32,1024]{2,1,0:T(8,128)(2,1)S(1)}, u32[]{:S(2)}, u32[]{:S(2)}) collective-permute-start(bf16[4,32,1024]{2,1,0:T(8,128)(2,1)S(1)} %collective-permute-done.4.refs_0_), channel_id=1, source_target_pairs={{0,224},{32,0},{64,32},{96,64},{128,96},{160,128},{192,160},{224,1... | collective-permute-start | bytes 786440 | tf_op jit(solution)/shard_map/ppermute | solution.py:18
  39.4 4.6 %collective-permute-done.5.refs_1_ = bf16[4,32,1024]{2,1,0:T(8,128)(2,1)S(1)} collective-permute-done((bf16[4,32,1024]{2,1,0:T(8,128)(2,1)}, bf16[4,32,1024]{2,1,0:T(8,128)(2,1)S(1)}, u32[]{:S(2)}, u32[]{:S(2)}) %collective-permute-start.5) | collective-permute-done | bytes 262176 | tf_op jit(solution)/shard_map/ppermute | solution.py:18
  45.5 6.0 %collective-permute-done.7.refs_3_ = bf16[4,32,1024]{2,1,0:T(8,128)(2,1)S(1)} collective-permute-done((bf16[4,32,1024]{2,1,0:T(8,128)(2,1)S(1)}, bf16[4,32,1024]{2,1,0:T(8,128)(2,1)S(1)}, u32[]{:S(2)}, u32[]{:S(2)}) %collective-permute-start.7) | collective-permute-done | bytes 262176 | tf_op jit(solution)/shard_map/ppermute | solution.py:18
  56.7 9.0 %all-to-all-start.1 = ((bf16[8,4,32,768]{3,2,1,0:T(8,128)(2,1)}), bf16[8,4,32,768]{3,2,1,0:T(8,128)(2,1)}, u32[]{:S(2)}, u32[]{:S(2)}) async-start(bf16[8,4,32,768]{3,2,1,0:T(8,128)(2,1)} %copy-done), calls=%async_computation.1 | async-start | bytes 3145728 | tf_op jit(solution)/shard_map/all_to_all | solution.py:153
  69.5 2.7 %collective-permute-start.14 = (bf16[4,4,32,512]{3,2,1,0:T(8,128)(2,1)}, bf16[4,4,32,512]{3,2,1,0:T(8,128)(2,1)}, u32[]{:S(2)}, u32[]{:S(2)}) collective-permute-start(bf16[4,4,32,512]{3,2,1,0:T(8,128)(2,1)} %shard_map.40.refs_5_), channel_id=1, source_target_pairs={{0,4},{4,8},{8,12},{12,0},{1,5},{5,9},{9,13},{13,1},{2,6},{6,10},{... | collective-permute-start | bytes 1572872 | tf_op jit(solution)/shard_map/ppermute | solution.py:18
  72.2 16.9 %collective-permute-done.10.refs_2_ = bf16[2,4,32,1024]{3,2,1,0:T(8,128)(2,1)} collective-permute-done((bf16[2,4,32,1024]{3,2,1,0:T(8,128)(2,1)}, bf16[2,4,32,1024]{3,2,1,0:T(8,128)(2,1)}, u32[]{:S(2)}, u32[]{:S(2)}) %collective-permute-start.10) | collective-permute-done | bytes 524320 | tf_op jit(solution)/shard_map/ppermute | solution.py:18
  89.1 6.3 %collective-permute-done.11.refs_3_ = bf16[2,4,32,1024]{3,2,1,0:T(8,128)(2,1)} collective-permute-done((bf16[2,4,32,1024]{3,2,1,0:T(8,128)(2,1)}, bf16[2,4,32,1024]{3,2,1,0:T(8,128)(2,1)}, u32[]{:S(2)}, u32[]{:S(2)}) %collective-permute-start.11) | collective-permute-done | bytes 524320 | tf_op jit(solution)/shard_map/ppermute | solution.py:18
  95.4 7.2 %all-to-all-done.1.amps = bf16[8,4,32,768]{3,2,1,0:T(8,128)(2,1)} async-done(((bf16[8,4,32,768]{3,2,1,0:T(8,128)(2,1)}), bf16[8,4,32,768]{3,2,1,0:T(8,128)(2,1)}, u32[]{:S(2)}, u32[]{:S(2)}) %all-to-all-start.1) | async-done | bytes 1572896 | tf_op jit(solution)/shard_map/all_to_all | solution.py:153
  107.3 3.6 %shard_map.44 = (f32[384,512]{1,0:T(8,128)S(1)}, f32[384,512]{1,0:T(8,128)S(1)}) custom-call(bf16[384,1024]{1,0:T(8,128)(2,1)S(1)} %get-tuple-element.68.a0, bf16[384,1024]{1,0:T(8,128)(2,1)S(1)} %collective-permute-done.16.a1, bf16[4,4,32,1024]{3,2,1,0:T(8,128)(2,1)S(1)} %shard_map.38.refs_0_, bf16[4,4,32,1024]{3,2,1,0:T(8,128)(2,1)S(1)} %collective-permute-done.8.refs_1_, ...), custom_call_target="tpu_custom_call" | custom-call | flops 1 | bytes 1 | tf_op jit(solution)/shard_map/pallas_call | solution.py:34
  112.6 2.2 %collective-permute-start.18 = (f16[384,512]{1,0:T(8,128)(2,1)S(1)}, f16[384,512]{1,0:T(8,128)(2,1)S(1)}, u32[]{:S(2)}, u32[]{:S(2)}) collective-permute-start(f16[384,512]{1,0:T(8,128)(2,1)S(1)} %convert_element_type.38), channel_id=1, source_target_pairs={{0,18},{2,16},{16,2},{18,0},{1,19},{3,17},{17,3},{19,1},{4,22},{6,... | collective-permute-start | bytes 1179656 | tf_op jit(solution)/shard_map/ppermute | solution.py:22
  114.8 3.6 %shard_map.43 = (f32[384,512]{1,0:T(8,128)S(1)}, f32[384,512]{1,0:T(8,128)S(1)}) custom-call(bf16[384,1024]{1,0:T(8,128)(2,1)S(1)} %get-tuple-element.57.a0, bf16[384,1024]{1,0:T(8,128)(2,1)S(1)} %collective-permute-done.13.a1, bf16[4,4,32,1024]{3,2,1,0:T(8,128)(2,1)S(1)} %shard_map.38.refs_0_, bf16[4,4,32,1024]{3,2,1,0:T(8,128)(2,1)S(1)} %collective-permute-done.8.refs_1_, ...), custom_call_target="tpu_custom_call" | custom-call | flops 1 | bytes 1 | tf_op jit(solution)/shard_map/pallas_call | solution.py:34
  121.4 5.3 %collective-permute-done.21.refs_7_ = bf16[2,4,32,512]{3,2,1,0:T(8,128)(2,1)S(1)} collective-permute-done((bf16[2,4,32,512]{3,2,1,0:T(8,128)(2,1)S(1)}, bf16[2,4,32,512]{3,2,1,0:T(8,128)(2,1)S(1)}, u32[]{:S(2)}, u32[]{:S(2)}) %collective-permute-start.21) | collective-permute-done | bytes 262176 | tf_op jit(solution)/shard_map/ppermute | solution.py:18
  126.7 2.8 %collective-permute-done.23.refs_8_ = bf16[2,4,32,512]{3,2,1,0:T(8,128)(2,1)S(1)} collective-permute-done((bf16[2,4,32,512]{3,2,1,0:T(8,128)(2,1)S(1)}, bf16[2,4,32,512]{3,2,1,0:T(8,128)(2,1)S(1)}, u32[]{:S(2)}, u32[]{:S(2)}) %collective-permute-start.23) | collective-permute-done | bytes 262176 | tf_op jit(solution)/shard_map/ppermute | solution.py:18
  129.6 3.0 %shard_map.46 = (f32[384,512]{1,0:T(8,128)S(1)}, f32[384,512]{1,0:T(8,128)S(1)}) custom-call(bf16[384,1024]{1,0:T(8,128)(2,1)S(1)} %get-tuple-element.68.a0, bf16[384,1024]{1,0:T(8,128)(2,1)S(1)} %collective-permute-done.16.a1, bf16[4,4,32,1024]{3,2,1,0:T(8,128)(2,1)S(1)} %shard_map.38.refs_0_, bf16[4,4,32,1024]{3,2,1,0:T(8,128)(2,1)S(1)} %collective-permute-done.8.refs_1_, ...), custom_call_target="tpu_custom_call" | custom-call | flops 1 | bytes 1 | tf_op jit(solution)/shard_map/pallas_call | solution.py:34
  134.2 2.2 %collective-permute-start.25 = (f16[384,512]{1,0:T(8,128)(2,1)S(1)}, f16[384,512]{1,0:T(8,128)(2,1)S(1)}, u32[]{:S(2)}, u32[]{:S(2)}) collective-permute-start(f16[384,512]{1,0:T(8,128)(2,1)S(1)} %convert_element_type.44), channel_id=1, source_target_pairs={{0,18},{2,16},{16,2},{18,0},{1,19},{3,17},{17,3},{19,1},{4,22},{6,... | collective-permute-start | bytes 1179656 | tf_op jit(solution)/shard_map/ppermute | solution.py:22
  136.4 3.0 %shard_map.45 = (f32[384,512]{1,0:T(8,128)S(1)}, f32[384,512]{1,0:T(8,128)S(1)}) custom-call(bf16[384,1024]{1,0:T(8,128)(2,1)S(1)} %get-tuple-element.57.a0, bf16[384,1024]{1,0:T(8,128)(2,1)S(1)} %collective-permute-done.13.a1, bf16[4,4,32,1024]{3,2,1,0:T(8,128)(2,1)S(1)} %shard_map.38.refs_0_, bf16[4,4,32,1024]{3,2,1,0:T(8,128)(2,1)S(1)} %collective-permute-done.8.refs_1_, ...), custom_call_target="tpu_custom_call" | custom-call | flops 1 | bytes 1 | tf_op jit(solution)/shard_map/pallas_call | solution.py:34
  140.4 3.3 %collective-permute-done.24 = f16[384,512]{1,0:T(8,128)(2,1)S(1)} collective-permute-done((f16[384,512]{1,0:T(8,128)(2,1)S(1)}, f16[384,512]{1,0:T(8,128)(2,1)S(1)}, u32[]{:S(2)}, u32[]{:S(2)}) %collective-permute-start.24) | collective-permute-done | bytes 393248 | tf_op jit(solution)/shard_map/ppermute | solution.py:18
  143.8 9.0 %collective-permute-done.25 = f16[384,512]{1,0:T(8,128)(2,1)S(1)} collective-permute-done((f16[384,512]{1,0:T(8,128)(2,1)S(1)}, f16[384,512]{1,0:T(8,128)(2,1)S(1)}, u32[]{:S(2)}, u32[]{:S(2)}) %collective-permute-start.25) | collective-permute-done | bytes 393248 | tf_op jit(solution)/shard_map/ppermute | solution.py:22
  (79 shorter events, 34.9 us)
Async XLA Ops:
  7.8 23.7 %all-to-all-start = ((bf16[4,8,32,768]{3,2,1,0:T(8,128)(2,1)}), bf16[4,8,32,768]{3,2,1,0:T(8,128)(2,1)S(1)}, u32[]{:S(2)}, u32[]{:S(2)}) async-start(bf16[4,8,32,768]{3,2,1,0:T(8,128)(2,1)} %copy-done.3), calls=%async_computation | async-start | bytes 3145728 | tf_op jit(solution)/shard_map/all_to_all | solution.py:150
  13.1 10.2 %collective-permute-start.1 = (bf16[4,32,1024]{2,1,0:T(8,128)(2,1)S(1)}, bf16[4,32,1024]{2,1,0:T(8,128)(2,1)S(1)}, u32[]{:S(2)}, u32[]{:S(2)}) collective-permute-start(bf16[4,32,1024]{2,1,0:T(8,128)(2,1)S(1)} %pad_maximum_fusion.refs_0_), channel_id=1, source_target_pairs={{0,32},{32,64},{64,96},{96,128},{128,160},{160,192},{192,224},{224... | collective-permute-start | bytes 786440 | tf_op jit(solution)/shard_map/ppermute | solution.py:18
  14.5 8.8 %collective-permute-start.2 = (bf16[4,32,1024]{2,1,0:T(8,128)(2,1)S(1)}, bf16[4,32,1024]{2,1,0:T(8,128)(2,1)S(1)}, u32[]{:S(2)}, u32[]{:S(2)}) collective-permute-start(bf16[4,32,1024]{2,1,0:T(8,128)(2,1)S(1)} %pad_maximum_fusion.refs_0_), channel_id=1, source_target_pairs={{0,224},{32,0},{64,32},{96,64},{128,96},{160,128},{192,160},{224,1... | collective-permute-start | bytes 786440 | tf_op jit(solution)/shard_map/ppermute | solution.py:18
  23.3 8.3 %collective-permute-start.4 = (bf16[4,32,1024]{2,1,0:T(8,128)(2,1)S(1)}, bf16[4,32,1024]{2,1,0:T(8,128)(2,1)S(1)}, u32[]{:S(2)}, u32[]{:S(2)}) collective-permute-start(bf16[4,32,1024]{2,1,0:T(8,128)(2,1)S(1)} %collective-permute-done.2.refs_2_), channel_id=1, source_target_pairs={{0,224},{32,0},{64,32},{96,64},{128,96},{160,128},{192,160},{224,1... | collective-permute-start | bytes 786440 | tf_op jit(solution)/shard_map/ppermute | solution.py:18
  32.7 22.0 %collective-permute-start.8 = (bf16[4,4,32,1024]{3,2,1,0:T(8,128)(2,1)S(1)}, bf16[4,4,32,1024]{3,2,1,0:T(8,128)(2,1)S(1)}, u32[]{:S(2)}, u32[]{:S(2)}) collective-permute-start(bf16[4,4,32,1024]{3,2,1,0:T(8,128)(2,1)S(1)} %shard_map.38.refs_0_), channel_id=1, source_target_pairs={{0,4},{4,8},{8,12},{12,0},{1,5},{5,9},{9,13},{13,1},{2,6},{6,10},{... | collective-permute-start | bytes 3145736 | tf_op jit(solution)/shard_map/ppermute | solution.py:18
  33.5 23.2 %collective-permute-start.9 = (bf16[4,4,32,1024]{3,2,1,0:T(8,128)(2,1)S(1)}, bf16[4,4,32,1024]{3,2,1,0:T(8,128)(2,1)S(1)}, u32[]{:S(2)}, u32[]{:S(2)}) collective-permute-start(bf16[4,4,32,1024]{3,2,1,0:T(8,128)(2,1)S(1)} %shard_map.38.refs_0_), channel_id=1, source_target_pairs={{0,12},{4,0},{8,4},{12,8},{1,13},{5,1},{9,5},{13,9},{2,14},{6,2},{... | collective-permute-start | bytes 3145736 | tf_op jit(solution)/shard_map/ppermute | solution.py:18
  34.7 9.2 %collective-permute-start.5 = (bf16[4,32,1024]{2,1,0:T(8,128)(2,1)}, bf16[4,32,1024]{2,1,0:T(8,128)(2,1)S(1)}, u32[]{:S(2)}, u32[]{:S(2)}) collective-permute-start(bf16[4,32,1024]{2,1,0:T(8,128)(2,1)} %copy-done.7), channel_id=1, source_target_pairs={{0,32},{32,64},{64,96},{96,128},{128,160},{160,192},{192,224},{224... | collective-permute-start | bytes 786440 | tf_op jit(solution)/shard_map/ppermute | solution.py:18
  35.4 10.0 %collective-permute-start.6 = (bf16[4,32,1024]{2,1,0:T(8,128)(2,1)S(1)}, bf16[4,32,1024]{2,1,0:T(8,128)(2,1)S(1)}, u32[]{:S(2)}, u32[]{:S(2)}) collective-permute-start(bf16[4,32,1024]{2,1,0:T(8,128)(2,1)S(1)} %collective-permute-done.4.refs_0_), channel_id=1, source_target_pairs={{0,224},{32,0},{64,32},{96,64},{128,96},{160,128},{192,160},{224,1... | collective-permute-start | bytes 786440 | tf_op jit(solution)/shard_map/ppermute | solution.py:18
  56.7 45.8 %all-to-all-start.1 = ((bf16[8,4,32,768]{3,2,1,0:T(8,128)(2,1)}), bf16[8,4,32,768]{3,2,1,0:T(8,128)(2,1)}, u32[]{:S(2)}, u32[]{:S(2)}) async-start(bf16[8,4,32,768]{3,2,1,0:T(8,128)(2,1)} %copy-done), calls=%async_computation.1 | async-start | bytes 3145728 | tf_op jit(solution)/shard_map/all_to_all | solution.py:153
  66.6 22.5 %collective-permute-start.10 = (bf16[2,4,32,1024]{3,2,1,0:T(8,128)(2,1)}, bf16[2,4,32,1024]{3,2,1,0:T(8,128)(2,1)}, u32[]{:S(2)}, u32[]{:S(2)}) collective-permute-start(bf16[2,4,32,1024]{3,2,1,0:T(8,128)(2,1)} %slice.12), channel_id=1, source_target_pairs={{0,4},{4,8},{8,12},{12,0},{1,5},{5,9},{9,13},{13,1},{2,6},{6,10},{... | collective-permute-start | bytes 1572872 | tf_op jit(solution)/shard_map/ppermute | solution.py:18
  67.7 27.6 %collective-permute-start.11 = (bf16[2,4,32,1024]{3,2,1,0:T(8,128)(2,1)}, bf16[2,4,32,1024]{3,2,1,0:T(8,128)(2,1)}, u32[]{:S(2)}, u32[]{:S(2)}) collective-permute-start(bf16[2,4,32,1024]{3,2,1,0:T(8,128)(2,1)} %slice.13), channel_id=1, source_target_pairs={{0,12},{4,0},{8,4},{12,8},{1,13},{5,1},{9,5},{13,9},{2,14},{6,2},{... | collective-permute-start | bytes 1572872 | tf_op jit(solution)/shard_map/ppermute | solution.py:18
  69.5 25.9 %collective-permute-start.12 = (bf16[4,4,32,512]{3,2,1,0:T(8,128)(2,1)}, bf16[4,4,32,512]{3,2,1,0:T(8,128)(2,1)}, u32[]{:S(2)}, u32[]{:S(2)}) collective-permute-start(bf16[4,4,32,512]{3,2,1,0:T(8,128)(2,1)} %shard_map.40.refs_5_), channel_id=1, source_target_pairs={{0,8},{4,12},{8,0},{12,4},{1,9},{5,13},{9,1},{13,5},{2,10},{6,14},... | collective-permute-start | bytes 1572872 | tf_op jit(solution)/shard_map/ppermute | solution.py:18
  69.5 35.7 %collective-permute-start.14 = (bf16[4,4,32,512]{3,2,1,0:T(8,128)(2,1)}, bf16[4,4,32,512]{3,2,1,0:T(8,128)(2,1)}, u32[]{:S(2)}, u32[]{:S(2)}) collective-permute-start(bf16[4,4,32,512]{3,2,1,0:T(8,128)(2,1)} %shard_map.40.refs_5_), channel_id=1, source_target_pairs={{0,4},{4,8},{8,12},{12,0},{1,5},{5,9},{9,13},{13,1},{2,6},{6,10},{... | collective-permute-start | bytes 1572872 | tf_op jit(solution)/shard_map/ppermute | solution.py:18
  72.2 33.0 %collective-permute-start.15 = (bf16[4,4,32,512]{3,2,1,0:T(8,128)(2,1)}, bf16[4,4,32,512]{3,2,1,0:T(8,128)(2,1)}, u32[]{:S(2)}, u32[]{:S(2)}) collective-permute-start(bf16[4,4,32,512]{3,2,1,0:T(8,128)(2,1)} %shard_map.40.refs_5_), channel_id=1, source_target_pairs={{0,12},{4,0},{8,4},{12,8},{1,13},{5,1},{9,5},{13,9},{2,14},{6,2},{... | collective-permute-start | bytes 1572872 | tf_op jit(solution)/shard_map/ppermute | solution.py:18
  104.7 10.1 %collective-permute-start.13 = (bf16[384,1024]{1,0:T(8,128)(2,1)S(1)}, bf16[384,1024]{1,0:T(8,128)(2,1)S(1)}, u32[]{:S(2)}, u32[]{:S(2)}) collective-permute-start(bf16[384,1024]{1,0:T(8,128)(2,1)S(1)} %get-tuple-element.57.a0), channel_id=1, source_target_pairs={{0,1},{1,0},{2,3},{3,2},{4,5},{5,4},{6,7},{7,6},{8,9},{9,8},{10,11... | collective-permute-start | bytes 2359304 | tf_op jit(solution)/shard_map/ppermute | solution.py:18
  105.2 14.0 %collective-permute-start.20 = (bf16[4,4,32,512]{3,2,1,0:T(8,128)(2,1)S(1)}, bf16[4,4,32,512]{3,2,1,0:T(8,128)(2,1)S(1)}, u32[]{:S(2)}, u32[]{:S(2)}) collective-permute-start(bf16[4,4,32,512]{3,2,1,0:T(8,128)(2,1)S(1)} %copy-done.5), channel_id=1, source_target_pairs={{0,4},{4,8},{8,12},{12,0},{1,5},{5,9},{9,13},{13,1},{2,6},{6,10},{... | collective-permute-start | bytes 1572872 | tf_op jit(solution)/shard_map/ppermute | solution.py:18
  105.8 15.3 %collective-permute-start.22 = (bf16[4,4,32,512]{3,2,1,0:T(8,128)(2,1)S(1)}, bf16[4,4,32,512]{3,2,1,0:T(8,128)(2,1)S(1)}, u32[]{:S(2)}, u32[]{:S(2)}) collective-permute-start(bf16[4,4,32,512]{3,2,1,0:T(8,128)(2,1)S(1)} %copy-done.5), channel_id=1, source_target_pairs={{0,12},{4,0},{8,4},{12,8},{1,13},{5,1},{9,5},{13,9},{2,14},{6,2},{... | collective-permute-start | bytes 1572872 | tf_op jit(solution)/shard_map/ppermute | solution.py:18
  111.0 28.5 %collective-permute-start.17 = (f16[384,512]{1,0:T(8,128)(2,1)S(1)}, f16[384,512]{1,0:T(8,128)(2,1)S(1)}, u32[]{:S(2)}, u32[]{:S(2)}) collective-permute-start(f16[384,512]{1,0:T(8,128)(2,1)S(1)} %convert_element_type.36), channel_id=1, source_target_pairs={{0,16},{16,0},{1,17},{17,1},{2,18},{18,2},{3,19},{19,3},{4,20},{20... | collective-permute-start | bytes 1179656 | tf_op jit(solution)/shard_map/ppermute | solution.py:18
  112.6 27.6 %collective-permute-start.18 = (f16[384,512]{1,0:T(8,128)(2,1)S(1)}, f16[384,512]{1,0:T(8,128)(2,1)S(1)}, u32[]{:S(2)}, u32[]{:S(2)}) collective-permute-start(f16[384,512]{1,0:T(8,128)(2,1)S(1)} %convert_element_type.38), channel_id=1, source_target_pairs={{0,18},{2,16},{16,2},{18,0},{1,19},{3,17},{17,3},{19,1},{4,22},{6,... | collective-permute-start | bytes 1179656 | tf_op jit(solution)/shard_map/ppermute | solution.py:22
  118.5 21.8 %collective-permute-start.19 = (f16[384,512]{1,0:T(8,128)(2,1)S(1)}, f16[384,512]{1,0:T(8,128)(2,1)S(1)}, u32[]{:S(2)}, u32[]{:S(2)}) collective-permute-start(f16[384,512]{1,0:T(8,128)(2,1)S(1)} %convert_element_type.40), channel_id=1, source_target_pairs={{0,2},{2,0},{1,3},{3,1},{4,6},{6,4},{5,7},{7,5},{8,10},{10,8},{9,1... | collective-permute-start | bytes 1179656 | tf_op jit(solution)/shard_map/ppermute | solution.py:18
  121.1 8.5 %collective-permute-start.23 = (bf16[2,4,32,512]{3,2,1,0:T(8,128)(2,1)S(1)}, bf16[2,4,32,512]{3,2,1,0:T(8,128)(2,1)S(1)}, u32[]{:S(2)}, u32[]{:S(2)}) collective-permute-start(bf16[2,4,32,512]{3,2,1,0:T(8,128)(2,1)S(1)} %slice.17), channel_id=1, source_target_pairs={{0,12},{4,0},{8,4},{12,8},{1,13},{5,1},{9,5},{13,9},{2,14},{6,2},{... | collective-permute-start | bytes 786440 | tf_op jit(solution)/shard_map/ppermute | solution.py:18
  132.6 11.2 %collective-permute-start.24 = (f16[384,512]{1,0:T(8,128)(2,1)S(1)}, f16[384,512]{1,0:T(8,128)(2,1)S(1)}, u32[]{:S(2)}, u32[]{:S(2)}) collective-permute-start(f16[384,512]{1,0:T(8,128)(2,1)S(1)} %convert_element_type.42), channel_id=1, source_target_pairs={{0,16},{16,0},{1,17},{17,1},{2,18},{18,2},{3,19},{19,3},{4,20},{20... | collective-permute-start | bytes 1179656 | tf_op jit(solution)/shard_map/ppermute | solution.py:18
  134.2 18.5 %collective-permute-start.25 = (f16[384,512]{1,0:T(8,128)(2,1)S(1)}, f16[384,512]{1,0:T(8,128)(2,1)S(1)}, u32[]{:S(2)}, u32[]{:S(2)}) collective-permute-start(f16[384,512]{1,0:T(8,128)(2,1)S(1)} %convert_element_type.44), channel_id=1, source_target_pairs={{0,18},{2,16},{16,2},{18,0},{1,19},{3,17},{17,3},{19,1},{4,22},{6,... | collective-permute-start | bytes 1179656 | tf_op jit(solution)/shard_map/ppermute | solution.py:22
  139.5 13.3 %collective-permute-start.26 = (f16[384,512]{1,0:T(8,128)(2,1)S(1)}, f16[384,512]{1,0:T(8,128)(2,1)S(1)}, u32[]{:S(2)}, u32[]{:S(2)}) collective-permute-start(f16[384,512]{1,0:T(8,128)(2,1)S(1)} %convert_element_type.46), channel_id=1, source_target_pairs={{0,2},{2,0},{1,3},{3,1},{4,6},{6,4},{5,7},{7,5},{8,10},{10,8},{9,1... | collective-permute-start | bytes 1179656 | tf_op jit(solution)/shard_map/ppermute | solution.py:18
  (14 other events, 61.8 us)

commit v4 on v3

--- a/solution.py
+++ b/solution.py
@@ -171,11 +171,12 @@
 
     near_two = beyond(near_up, near_down)
     near = [near, near_up, *near_two, near_down]
-    far = [[own[0], *[shift(own[0], "y", d) for d in (1, 2, 3)]]]
-    far[0][1], far[0][3], own[1] = tie(far[0][1], far[0][3], own[1])
+    first = along_y(own[0])
+    first, own[1] = tie(first, own[1])
+    far = [[own[0], first[0], *beyond(*first), first[1]]]
     ends = along_y(own[1])
     far.append([own[1], ends[0], *beyond(*ends), ends[1]])
-    amps, near, far[0][2] = tie(amps, near, far[0][2])
+    amps, near, far[0] = tie(amps, near, far[0])
     place = jnp.stack([z, y]).astype(jnp.int32)
     shape = jax.ShapeDtypeStruct((rows, NZ * NY * cds), kind)
     theirs, mine = call(turn_kernel, [shape, shape], [amps], place)

time: 155 us -> 155 us (level)
  local copies, waits for them, and re-layouts: 9.24 us -> 13.4 us
  waiting for transfers between devices: 75.1 us -> 71.5 us
  Pallas kernels: 16.4 us -> 14.5 us
    ppermute x25 -> x26, waiting for transfers between devices: 59 us -> 54.6 us  [shift(): lax.ppermute(value, axis, [(i, (i + by) % size) for i in range(size)])]
    unnamed x18 -> x30, local copies, waits for them, and re-layouts: 6.55 us -> 9.15 us
    pallas_call x10, Pallas kernels: 16.4 us -> 14.5 us  [call(): pl.pallas_call(kernel, out_shape=out_shape, in_specs=[smem] * len(first)...]
    slice x4 -> x6, local copies, waits for them, and re-layouts: 1.74 us -> 3.26 us  [beyond(): return (shift(up[:half], 'y', 1), shift(down[half:], 'y', -1))]
    ppermute x25 -> x26, starting transfers between devices: 32.6 us -> 33.9 us  [shift(): lax.ppermute(value, axis, [(i, (i + by) % size) for i in range(size)])]
  transfers between devices with their start and end apart: 29 -> 30, of which waited for: 14 -> 19; matrix products, arithmetic and copies ran while one was open for 2% -> 3% of each run, Pallas kernels for 11% -> 8%
where the time goes in v4:
time: 155 us; the launch traced here: 154 us
  waiting for transfers between devices  71.5 us (46%)
  starting transfers between devices  52.5 us (34%)
  Pallas kernels  14.5 us (9%)
  local copies, waits for them, and re-layouts  13.4 us (9%)
  other arithmetic  2.28 us (1%)
    ppermute x26, waiting for transfers between devices, shift(): lax.ppermute(value, axis, [(i, (i + by) % size) for i in range(size)])  54.6 us
    ppermute x26, starting transfers between devices, shift(): lax.ppermute(value, axis, [(i, (i + by) % size) for i in range(size)])  33.9 us
    pallas_call x10, Pallas kernels, call(): pl.pallas_call(kernel, out_shape=out_shape, in_specs=[smem] * len(first)...  14.5 us
    unnamed x30, local copies, waits for them, and re-layouts  9.15 us
    all_to_all x1, starting transfers between devices, along_z(): return lax.all_to_all(amps, 'z', split_axis=0, concat_axis=0, tiled=True)  9 us
    ppermute x2, waiting for transfers between devices, across(): return lax.ppermute(value, ('x_lo', 'x_hi'), [(i, 3 - i) for i in range(4)])  8.93 us
    all_to_all x1, waiting for transfers between devices, along_z(): return lax.all_to_all(amps, 'z', split_axis=0, concat_axis=0, tiled=True)  8.02 us
    all_to_all x1, starting transfers between devices, per_device(): got = lax.all_to_all(cut, 'y', split_axis=0, concat_axis=0, tiled=True)  5.24 us
  transfers between devices with their start and end apart: 30, of which 19 were waited for; matrix products, arithmetic and copies ran while one was open for 3% of the time, Pallas kernels for 8%

profile of v4, /device:TPU:24, one launch (start us, length us, event | category | flops | bytes accessed | tf_op | source)
XLA Modules:
  0.0 154.4 jit_solution(18156025367315197840)
XLA Ops:
  1.0 3.1 %collective-permute-start = (bf16[2,32,1024]{2,1,0:T(8,128)(2,1)S(1)}, bf16[2,32,1024]{2,1,0:T(8,128)(2,1)S(1)}, u32[]{:S(2)}, u32[]{:S(2)}) collective-permute-start(bf16[2,32,1024]{2,1,0:T(8,128)(2,1)S(1)} %pad_maximum_fusion.1), channel_id=1, source_target_pairs={{0,2},{2,0},{1,3},{3,1},{4,6},{6,4},{5,7},{7,5},{8,10},{10,8},{9,1... | collective-permute-start | bytes 393224 | tf_op jit(solution)/shard_map/ppermute | solution.py:18
  7.8 5.2 %all-to-all-start = ((bf16[4,8,32,768]{3,2,1,0:T(8,128)(2,1)}), bf16[4,8,32,768]{3,2,1,0:T(8,128)(2,1)S(1)}, u32[]{:S(2)}, u32[]{:S(2)}) async-start(bf16[4,8,32,768]{3,2,1,0:T(8,128)(2,1)} %copy-done.3), calls=%async_computation | async-start | bytes 3145728 | tf_op jit(solution)/shard_map/all_to_all | solution.py:150
  14.5 3.9 %collective-permute-start.2 = (bf16[4,32,1024]{2,1,0:T(8,128)(2,1)S(1)}, bf16[4,32,1024]{2,1,0:T(8,128)(2,1)S(1)}, u32[]{:S(2)}, u32[]{:S(2)}) collective-permute-start(bf16[4,32,1024]{2,1,0:T(8,128)(2,1)S(1)} %pad_maximum_fusion.refs_0_), channel_id=1, source_target_pairs={{0,224},{32,0},{64,32},{96,64},{128,96},{160,128},{192,160},{224,1... | collective-permute-start | bytes 786440 | tf_op jit(solution)/shard_map/ppermute | solution.py:18
  18.4 4.9 %collective-permute-done.1.refs_1_ = bf16[4,32,1024]{2,1,0:T(8,128)(2,1)S(1)} collective-permute-done((bf16[4,32,1024]{2,1,0:T(8,128)(2,1)S(1)}, bf16[4,32,1024]{2,1,0:T(8,128)(2,1)S(1)}, u32[]{:S(2)}, u32[]{:S(2)}) %collective-permute-start.1) | collective-permute-done | bytes 262176 | tf_op jit(solution)/shard_map/ppermute | solution.py:18
  23.3 3.2 %collective-permute-start.4 = (bf16[4,32,1024]{2,1,0:T(8,128)(2,1)S(1)}, bf16[4,32,1024]{2,1,0:T(8,128)(2,1)S(1)}, u32[]{:S(2)}, u32[]{:S(2)}) collective-permute-start(bf16[4,32,1024]{2,1,0:T(8,128)(2,1)S(1)} %collective-permute-done.2.refs_2_), channel_id=1, source_target_pairs={{0,224},{32,0},{64,32},{96,64},{128,96},{160,128},{192,160},{224,1... | collective-permute-start | bytes 786440 | tf_op jit(solution)/shard_map/ppermute | solution.py:18
  26.5 4.3 %collective-permute-done.3.refs_3_ = bf16[4,32,1024]{2,1,0:T(8,128)(2,1)S(1)} collective-permute-done((bf16[4,32,1024]{2,1,0:T(8,128)(2,1)S(1)}, bf16[4,32,1024]{2,1,0:T(8,128)(2,1)S(1)}, u32[]{:S(2)}, u32[]{:S(2)}) %collective-permute-start.3) | collective-permute-done | bytes 262176 | tf_op jit(solution)/shard_map/ppermute | solution.py:18
  35.4 3.9 %collective-permute-start.6 = (bf16[4,32,1024]{2,1,0:T(8,128)(2,1)S(1)}, bf16[4,32,1024]{2,1,0:T(8,128)(2,1)S(1)}, u32[]{:S(2)}, u32[]{:S(2)}) collective-permute-start(bf16[4,32,1024]{2,1,0:T(8,128)(2,1)S(1)} %collective-permute-done.4.refs_0_), channel_id=1, source_target_pairs={{0,224},{32,0},{64,32},{96,64},{128,96},{160,128},{192,160},{224,1... | collective-permute-start | bytes 786440 | tf_op jit(solution)/shard_map/ppermute | solution.py:18
  39.4 4.6 %collective-permute-done.5.refs_1_ = bf16[4,32,1024]{2,1,0:T(8,128)(2,1)S(1)} collective-permute-done((bf16[4,32,1024]{2,1,0:T(8,128)(2,1)}, bf16[4,32,1024]{2,1,0:T(8,128)(2,1)S(1)}, u32[]{:S(2)}, u32[]{:S(2)}) %collective-permute-start.5) | collective-permute-done | bytes 262176 | tf_op jit(solution)/shard_map/ppermute | solution.py:18
  45.5 6.0 %collective-permute-done.7.refs_3_ = bf16[4,32,1024]{2,1,0:T(8,128)(2,1)S(1)} collective-permute-done((bf16[4,32,1024]{2,1,0:T(8,128)(2,1)S(1)}, bf16[4,32,1024]{2,1,0:T(8,128)(2,1)S(1)}, u32[]{:S(2)}, u32[]{:S(2)}) %collective-permute-start.7) | collective-permute-done | bytes 262176 | tf_op jit(solution)/shard_map/ppermute | solution.py:18
  54.7 2.1 %collective-permute-done.9.refs_4_ = bf16[4,4,32,1024]{3,2,1,0:T(8,128)(2,1)S(1)} collective-permute-done((bf16[4,4,32,1024]{3,2,1,0:T(8,128)(2,1)S(1)}, bf16[4,4,32,1024]{3,2,1,0:T(8,128)(2,1)S(1)}, u32[]{:S(2)}, u32[]{:S(2)}) %collective-permute-start.9) | collective-permute-done | bytes 1048608 | tf_op jit(solution)/shard_map/ppermute | solution.py:18
  56.7 9.0 %all-to-all-start.1 = ((bf16[8,4,32,768]{3,2,1,0:T(8,128)(2,1)}), bf16[8,4,32,768]{3,2,1,0:T(8,128)(2,1)}, u32[]{:S(2)}, u32[]{:S(2)}) async-start(bf16[8,4,32,768]{3,2,1,0:T(8,128)(2,1)} %copy-done), calls=%async_computation.1 | async-start | bytes 3145728 | tf_op jit(solution)/shard_map/all_to_all | solution.py:153
  71.5 9.3 %collective-permute-done.12.refs_6_ = bf16[4,4,32,512]{3,2,1,0:T(8,128)(2,1)S(1)} collective-permute-done((bf16[4,4,32,512]{3,2,1,0:T(8,128)(2,1)}, bf16[4,4,32,512]{3,2,1,0:T(8,128)(2,1)S(1)}, u32[]{:S(2)}, u32[]{:S(2)}) %collective-permute-start.12) | collective-permute-done | bytes 524320 | tf_op jit(solution)/shard_map/ppermute | solution.py:18
  86.7 3.5 %collective-permute-done.10.refs_2_ = bf16[2,4,32,1024]{3,2,1,0:T(8,128)(2,1)} collective-permute-done((bf16[2,4,32,1024]{3,2,1,0:T(8,128)(2,1)}, bf16[2,4,32,1024]{3,2,1,0:T(8,128)(2,1)}, u32[]{:S(2)}, u32[]{:S(2)}) %collective-permute-start.10) | collective-permute-done | bytes 524320 | tf_op jit(solution)/shard_map/ppermute | solution.py:18
  94.5 8.0 %all-to-all-done.1.amps = bf16[8,4,32,768]{3,2,1,0:T(8,128)(2,1)} async-done(((bf16[8,4,32,768]{3,2,1,0:T(8,128)(2,1)}), bf16[8,4,32,768]{3,2,1,0:T(8,128)(2,1)}, u32[]{:S(2)}, u32[]{:S(2)}) %all-to-all-start.1) | async-done | bytes 1572896 | tf_op jit(solution)/shard_map/all_to_all | solution.py:153
  108.3 3.0 %shard_map.44 = (f32[384,512]{1,0:T(8,128)S(1)}, f32[384,512]{1,0:T(8,128)S(1)}) custom-call(bf16[384,1024]{1,0:T(8,128)(2,1)S(1)} %get-tuple-element.76.a0, bf16[384,1024]{1,0:T(8,128)(2,1)S(1)} %collective-permute-done.17.a1, bf16[4,4,32,1024]{3,2,1,0:T(8,128)(2,1)S(1)} %shard_map.38.refs_0_, bf16[4,4,32,1024]{3,2,1,0:T(8,128)(2,1)S(1)} %collective-permute-done.8.refs_1_, ...), custom_call_target="tpu_custom_call" | custom-call | flops 1 | bytes 1 | tf_op jit(solution)/shard_map/pallas_call | solution.py:34
  113.0 2.2 %collective-permute-start.19 = (f16[384,512]{1,0:T(8,128)(2,1)S(1)}, f16[384,512]{1,0:T(8,128)(2,1)S(1)}, u32[]{:S(2)}, u32[]{:S(2)}) collective-permute-start(f16[384,512]{1,0:T(8,128)(2,1)S(1)} %convert_element_type.38), channel_id=1, source_target_pairs={{0,18},{2,16},{16,2},{18,0},{1,19},{3,17},{17,3},{19,1},{4,22},{6,... | collective-permute-start | bytes 1179656 | tf_op jit(solution)/shard_map/ppermute | solution.py:22
  115.2 3.0 %shard_map.43 = (f32[384,512]{1,0:T(8,128)S(1)}, f32[384,512]{1,0:T(8,128)S(1)}) custom-call(bf16[384,1024]{1,0:T(8,128)(2,1)S(1)} %get-tuple-element.64.a0, bf16[384,1024]{1,0:T(8,128)(2,1)S(1)} %collective-permute-done.16.a1, bf16[4,4,32,1024]{3,2,1,0:T(8,128)(2,1)S(1)} %shard_map.38.refs_0_, bf16[4,4,32,1024]{3,2,1,0:T(8,128)(2,1)S(1)} %collective-permute-done.8.refs_1_, ...), custom_call_target="tpu_custom_call" | custom-call | flops 1 | bytes 1 | tf_op jit(solution)/shard_map/pallas_call | solution.py:34
  121.4 5.3 %collective-permute-done.22.refs_7_ = bf16[2,4,32,512]{3,2,1,0:T(8,128)(2,1)S(1)} collective-permute-done((bf16[2,4,32,512]{3,2,1,0:T(8,128)(2,1)S(1)}, bf16[2,4,32,512]{3,2,1,0:T(8,128)(2,1)S(1)}, u32[]{:S(2)}, u32[]{:S(2)}) %collective-permute-start.22) | collective-permute-done | bytes 262176 | tf_op jit(solution)/shard_map/ppermute | solution.py:18
  126.7 2.8 %collective-permute-done.24.refs_8_ = bf16[2,4,32,512]{3,2,1,0:T(8,128)(2,1)S(1)} collective-permute-done((bf16[2,4,32,512]{3,2,1,0:T(8,128)(2,1)S(1)}, bf16[2,4,32,512]{3,2,1,0:T(8,128)(2,1)S(1)}, u32[]{:S(2)}, u32[]{:S(2)}) %collective-permute-start.24) | collective-permute-done | bytes 262176 | tf_op jit(solution)/shard_map/ppermute | solution.py:18
  129.5 3.0 %shard_map.46 = (f32[384,512]{1,0:T(8,128)S(1)}, f32[384,512]{1,0:T(8,128)S(1)}) custom-call(bf16[384,1024]{1,0:T(8,128)(2,1)S(1)} %get-tuple-element.76.a0, bf16[384,1024]{1,0:T(8,128)(2,1)S(1)} %collective-permute-done.17.a1, bf16[4,4,32,1024]{3,2,1,0:T(8,128)(2,1)S(1)} %shard_map.38.refs_0_, bf16[4,4,32,1024]{3,2,1,0:T(8,128)(2,1)S(1)} %collective-permute-done.8.refs_1_, ...), custom_call_target="tpu_custom_call" | custom-call | flops 1 | bytes 1 | tf_op jit(solution)/shard_map/pallas_call | solution.py:34
  134.2 2.2 %collective-permute-start.26 = (f16[384,512]{1,0:T(8,128)(2,1)S(1)}, f16[384,512]{1,0:T(8,128)(2,1)S(1)}, u32[]{:S(2)}, u32[]{:S(2)}) collective-permute-start(f16[384,512]{1,0:T(8,128)(2,1)S(1)} %convert_element_type.44), channel_id=1, source_target_pairs={{0,18},{2,16},{16,2},{18,0},{1,19},{3,17},{17,3},{19,1},{4,22},{6,... | collective-permute-start | bytes 1179656 | tf_op jit(solution)/shard_map/ppermute | solution.py:22
  136.4 3.0 %shard_map.45 = (f32[384,512]{1,0:T(8,128)S(1)}, f32[384,512]{1,0:T(8,128)S(1)}) custom-call(bf16[384,1024]{1,0:T(8,128)(2,1)S(1)} %get-tuple-element.64.a0, bf16[384,1024]{1,0:T(8,128)(2,1)S(1)} %collective-permute-done.16.a1, bf16[4,4,32,1024]{3,2,1,0:T(8,128)(2,1)S(1)} %shard_map.38.refs_0_, bf16[4,4,32,1024]{3,2,1,0:T(8,128)(2,1)S(1)} %collective-permute-done.8.refs_1_, ...), custom_call_target="tpu_custom_call" | custom-call | flops 1 | bytes 1 | tf_op jit(solution)/shard_map/pallas_call | solution.py:34
  140.4 3.4 %collective-permute-done.25 = f16[384,512]{1,0:T(8,128)(2,1)S(1)} collective-permute-done((f16[384,512]{1,0:T(8,128)(2,1)S(1)}, f16[384,512]{1,0:T(8,128)(2,1)S(1)}, u32[]{:S(2)}, u32[]{:S(2)}) %collective-permute-start.25) | collective-permute-done | bytes 393248 | tf_op jit(solution)/shard_map/ppermute | solution.py:18
  143.8 8.9 %collective-permute-done.26 = f16[384,512]{1,0:T(8,128)(2,1)S(1)} collective-permute-done((f16[384,512]{1,0:T(8,128)(2,1)S(1)}, f16[384,512]{1,0:T(8,128)(2,1)S(1)}, u32[]{:S(2)}, u32[]{:S(2)}) %collective-permute-start.26) | collective-permute-done | bytes 393248 | tf_op jit(solution)/shard_map/ppermute | solution.py:22
  (95 shorter events, 46.1 us)
Async XLA Ops:
  7.8 23.7 %all-to-all-start = ((bf16[4,8,32,768]{3,2,1,0:T(8,128)(2,1)}), bf16[4,8,32,768]{3,2,1,0:T(8,128)(2,1)S(1)}, u32[]{:S(2)}, u32[]{:S(2)}) async-start(bf16[4,8,32,768]{3,2,1,0:T(8,128)(2,1)} %copy-done.3), calls=%async_computation | async-start | bytes 3145728 | tf_op jit(solution)/shard_map/all_to_all | solution.py:150
  13.1 10.2 %collective-permute-start.1 = (bf16[4,32,1024]{2,1,0:T(8,128)(2,1)S(1)}, bf16[4,32,1024]{2,1,0:T(8,128)(2,1)S(1)}, u32[]{:S(2)}, u32[]{:S(2)}) collective-permute-start(bf16[4,32,1024]{2,1,0:T(8,128)(2,1)S(1)} %pad_maximum_fusion.refs_0_), channel_id=1, source_target_pairs={{0,32},{32,64},{64,96},{96,128},{128,160},{160,192},{192,224},{224... | collective-permute-start | bytes 786440 | tf_op jit(solution)/shard_map/ppermute | solution.py:18
  14.5 8.8 %collective-permute-start.2 = (bf16[4,32,1024]{2,1,0:T(8,128)(2,1)S(1)}, bf16[4,32,1024]{2,1,0:T(8,128)(2,1)S(1)}, u32[]{:S(2)}, u32[]{:S(2)}) collective-permute-start(bf16[4,32,1024]{2,1,0:T(8,128)(2,1)S(1)} %pad_maximum_fusion.refs_0_), channel_id=1, source_target_pairs={{0,224},{32,0},{64,32},{96,64},{128,96},{160,128},{192,160},{224,1... | collective-permute-start | bytes 786440 | tf_op jit(solution)/shard_map/ppermute | solution.py:18
  32.7 22.0 %collective-permute-start.8 = (bf16[4,4,32,1024]{3,2,1,0:T(8,128)(2,1)S(1)}, bf16[4,4,32,1024]{3,2,1,0:T(8,128)(2,1)S(1)}, u32[]{:S(2)}, u32[]{:S(2)}) collective-permute-start(bf16[4,4,32,1024]{3,2,1,0:T(8,128)(2,1)S(1)} %shard_map.38.refs_0_), channel_id=1, source_target_pairs={{0,4},{4,8},{8,12},{12,0},{1,5},{5,9},{9,13},{13,1},{2,6},{6,10},{... | collective-permute-start | bytes 3145736 | tf_op jit(solution)/shard_map/ppermute | solution.py:18
  33.5 23.2 %collective-permute-start.9 = (bf16[4,4,32,1024]{3,2,1,0:T(8,128)(2,1)S(1)}, bf16[4,4,32,1024]{3,2,1,0:T(8,128)(2,1)S(1)}, u32[]{:S(2)}, u32[]{:S(2)}) collective-permute-start(bf16[4,4,32,1024]{3,2,1,0:T(8,128)(2,1)S(1)} %shard_map.38.refs_0_), channel_id=1, source_target_pairs={{0,12},{4,0},{8,4},{12,8},{1,13},{5,1},{9,5},{13,9},{2,14},{6,2},{... | collective-permute-start | bytes 3145736 | tf_op jit(solution)/shard_map/ppermute | solution.py:18
  34.7 9.2 %collective-permute-start.5 = (bf16[4,32,1024]{2,1,0:T(8,128)(2,1)}, bf16[4,32,1024]{2,1,0:T(8,128)(2,1)S(1)}, u32[]{:S(2)}, u32[]{:S(2)}) collective-permute-start(bf16[4,32,1024]{2,1,0:T(8,128)(2,1)} %copy-done.13), channel_id=1, source_target_pairs={{0,32},{32,64},{64,96},{96,128},{128,160},{160,192},{192,224},{224... | collective-permute-start | bytes 786440 | tf_op jit(solution)/shard_map/ppermute | solution.py:18
  35.4 10.0 %collective-permute-start.6 = (bf16[4,32,1024]{2,1,0:T(8,128)(2,1)S(1)}, bf16[4,32,1024]{2,1,0:T(8,128)(2,1)S(1)}, u32[]{:S(2)}, u32[]{:S(2)}) collective-permute-start(bf16[4,32,1024]{2,1,0:T(8,128)(2,1)S(1)} %collective-permute-done.4.refs_0_), channel_id=1, source_target_pairs={{0,224},{32,0},{64,32},{96,64},{128,96},{160,128},{192,160},{224,1... | collective-permute-start | bytes 786440 | tf_op jit(solution)/shard_map/ppermute | solution.py:18
  56.7 45.8 %all-to-all-start.1 = ((bf16[8,4,32,768]{3,2,1,0:T(8,128)(2,1)}), bf16[8,4,32,768]{3,2,1,0:T(8,128)(2,1)}, u32[]{:S(2)}, u32[]{:S(2)}) async-start(bf16[8,4,32,768]{3,2,1,0:T(8,128)(2,1)} %copy-done), calls=%async_computation.1 | async-start | bytes 3145728 | tf_op jit(solution)/shard_map/all_to_all | solution.py:153
  65.7 15.1 %collective-permute-start.12 = (bf16[4,4,32,512]{3,2,1,0:T(8,128)(2,1)}, bf16[4,4,32,512]{3,2,1,0:T(8,128)(2,1)S(1)}, u32[]{:S(2)}, u32[]{:S(2)}) collective-permute-start(bf16[4,4,32,512]{3,2,1,0:T(8,128)(2,1)} %copy-done.6), channel_id=1, source_target_pairs={{0,4},{4,8},{8,12},{12,0},{1,5},{5,9},{9,13},{13,1},{2,6},{6,10},{... | collective-permute-start | bytes 1572872 | tf_op jit(solution)/shard_map/ppermute | solution.py:18
  66.0 16.3 %collective-permute-start.13 = (bf16[4,4,32,512]{3,2,1,0:T(8,128)(2,1)}, bf16[4,4,32,512]{3,2,1,0:T(8,128)(2,1)S(1)}, u32[]{:S(2)}, u32[]{:S(2)}) collective-permute-start(bf16[4,4,32,512]{3,2,1,0:T(8,128)(2,1)} %copy-done.6), channel_id=1, source_target_pairs={{0,12},{4,0},{8,4},{12,8},{1,13},{5,1},{9,5},{13,9},{2,14},{6,2},{... | collective-permute-start | bytes 1572872 | tf_op jit(solution)/shard_map/ppermute | solution.py:18
  68.6 21.6 %collective-permute-start.10 = (bf16[2,4,32,1024]{3,2,1,0:T(8,128)(2,1)}, bf16[2,4,32,1024]{3,2,1,0:T(8,128)(2,1)}, u32[]{:S(2)}, u32[]{:S(2)}) collective-permute-start(bf16[2,4,32,1024]{3,2,1,0:T(8,128)(2,1)} %slice.18), channel_id=1, source_target_pairs={{0,4},{4,8},{8,12},{12,0},{1,5},{5,9},{9,13},{13,1},{2,6},{6,10},{... | collective-permute-start | bytes 1572872 | tf_op jit(solution)/shard_map/ppermute | solution.py:18
  71.0 20.7 %collective-permute-start.11 = (bf16[2,4,32,1024]{3,2,1,0:T(8,128)(2,1)}, bf16[2,4,32,1024]{3,2,1,0:T(8,128)(2,1)}, u32[]{:S(2)}, u32[]{:S(2)}) collective-permute-start(bf16[2,4,32,1024]{3,2,1,0:T(8,128)(2,1)} %slice.19), channel_id=1, source_target_pairs={{0,12},{4,0},{8,4},{12,8},{1,13},{5,1},{9,5},{13,9},{2,14},{6,2},{... | collective-permute-start | bytes 1572872 | tf_op jit(solution)/shard_map/ppermute | solution.py:18
  83.9 9.0 %collective-permute-start.14 = (bf16[2,4,32,512]{3,2,1,0:T(8,128)(2,1)}, bf16[2,4,32,512]{3,2,1,0:T(8,128)(2,1)S(1)}, u32[]{:S(2)}, u32[]{:S(2)}) collective-permute-start(bf16[2,4,32,512]{3,2,1,0:T(8,128)(2,1)} %slice.20), channel_id=1, source_target_pairs={{0,4},{4,8},{8,12},{12,0},{1,5},{5,9},{9,13},{13,1},{2,6},{6,10},{... | collective-permute-start | bytes 786440 | tf_op jit(solution)/shard_map/ppermute | solution.py:18
  84.6 9.9 %collective-permute-start.15 = (bf16[2,4,32,512]{3,2,1,0:T(8,128)(2,1)}, bf16[2,4,32,512]{3,2,1,0:T(8,128)(2,1)}, u32[]{:S(2)}, u32[]{:S(2)}) collective-permute-start(bf16[2,4,32,512]{3,2,1,0:T(8,128)(2,1)} %slice.21), channel_id=1, source_target_pairs={{0,12},{4,0},{8,4},{12,8},{1,13},{5,1},{9,5},{13,9},{2,14},{6,2},{... | collective-permute-start | bytes 786440 | tf_op jit(solution)/shard_map/ppermute | solution.py:18
  104.7 10.5 %collective-permute-start.16 = (bf16[384,1024]{1,0:T(8,128)(2,1)S(1)}, bf16[384,1024]{1,0:T(8,128)(2,1)S(1)}, u32[]{:S(2)}, u32[]{:S(2)}) collective-permute-start(bf16[384,1024]{1,0:T(8,128)(2,1)S(1)} %get-tuple-element.64.a0), channel_id=1, source_target_pairs={{0,1},{1,0},{2,3},{3,2},{4,5},{5,4},{6,7},{7,6},{8,9},{9,8},{10,11... | collective-permute-start | bytes 2359304 | tf_op jit(solution)/shard_map/ppermute | solution.py:18
  105.2 13.9 %collective-permute-start.21 = (bf16[4,4,32,512]{3,2,1,0:T(8,128)(2,1)S(1)}, bf16[4,4,32,512]{3,2,1,0:T(8,128)(2,1)S(1)}, u32[]{:S(2)}, u32[]{:S(2)}) collective-permute-start(bf16[4,4,32,512]{3,2,1,0:T(8,128)(2,1)S(1)} %copy-done.5), channel_id=1, source_target_pairs={{0,4},{4,8},{8,12},{12,0},{1,5},{5,9},{9,13},{13,1},{2,6},{6,10},{... | collective-permute-start | bytes 1572872 | tf_op jit(solution)/shard_map/ppermute | solution.py:18
  105.8 15.2 %collective-permute-start.23 = (bf16[4,4,32,512]{3,2,1,0:T(8,128)(2,1)S(1)}, bf16[4,4,32,512]{3,2,1,0:T(8,128)(2,1)S(1)}, u32[]{:S(2)}, u32[]{:S(2)}) collective-permute-start(bf16[4,4,32,512]{3,2,1,0:T(8,128)(2,1)S(1)} %copy-done.5), channel_id=1, source_target_pairs={{0,12},{4,0},{8,4},{12,8},{1,13},{5,1},{9,5},{13,9},{2,14},{6,2},{... | collective-permute-start | bytes 1572872 | tf_op jit(solution)/shard_map/ppermute | solution.py:18
  111.4 28.0 %collective-permute-start.18 = (f16[384,512]{1,0:T(8,128)(2,1)S(1)}, f16[384,512]{1,0:T(8,128)(2,1)S(1)}, u32[]{:S(2)}, u32[]{:S(2)}) collective-permute-start(f16[384,512]{1,0:T(8,128)(2,1)S(1)} %convert_element_type.36), channel_id=1, source_target_pairs={{0,16},{16,0},{1,17},{17,1},{2,18},{18,2},{3,19},{19,3},{4,20},{20... | collective-permute-start | bytes 1179656 | tf_op jit(solution)/shard_map/ppermute | solution.py:18
  113.0 27.1 %collective-permute-start.19 = (f16[384,512]{1,0:T(8,128)(2,1)S(1)}, f16[384,512]{1,0:T(8,128)(2,1)S(1)}, u32[]{:S(2)}, u32[]{:S(2)}) collective-permute-start(f16[384,512]{1,0:T(8,128)(2,1)S(1)} %convert_element_type.38), channel_id=1, source_target_pairs={{0,18},{2,16},{16,2},{18,0},{1,19},{3,17},{17,3},{19,1},{4,22},{6,... | collective-permute-start | bytes 1179656 | tf_op jit(solution)/shard_map/ppermute | solution.py:22
  118.3 21.9 %collective-permute-start.20 = (f16[384,512]{1,0:T(8,128)(2,1)S(1)}, f16[384,512]{1,0:T(8,128)(2,1)S(1)}, u32[]{:S(2)}, u32[]{:S(2)}) collective-permute-start(f16[384,512]{1,0:T(8,128)(2,1)S(1)} %convert_element_type.40), channel_id=1, source_target_pairs={{0,2},{2,0},{1,3},{3,1},{4,6},{6,4},{5,7},{7,5},{8,10},{10,8},{9,1... | collective-permute-start | bytes 1179656 | tf_op jit(solution)/shard_map/ppermute | solution.py:18
  121.0 8.5 %collective-permute-start.24 = (bf16[2,4,32,512]{3,2,1,0:T(8,128)(2,1)S(1)}, bf16[2,4,32,512]{3,2,1,0:T(8,128)(2,1)S(1)}, u32[]{:S(2)}, u32[]{:S(2)}) collective-permute-start(bf16[2,4,32,512]{3,2,1,0:T(8,128)(2,1)S(1)} %slice.25), channel_id=1, source_target_pairs={{0,12},{4,0},{8,4},{12,8},{1,13},{5,1},{9,5},{13,9},{2,14},{6,2},{... | collective-permute-start | bytes 786440 | tf_op jit(solution)/shard_map/ppermute | solution.py:18
  132.6 11.2 %collective-permute-start.25 = (f16[384,512]{1,0:T(8,128)(2,1)S(1)}, f16[384,512]{1,0:T(8,128)(2,1)S(1)}, u32[]{:S(2)}, u32[]{:S(2)}) collective-permute-start(f16[384,512]{1,0:T(8,128)(2,1)S(1)} %convert_element_type.42), channel_id=1, source_target_pairs={{0,16},{16,0},{1,17},{17,1},{2,18},{18,2},{3,19},{19,3},{4,20},{20... | collective-permute-start | bytes 1179656 | tf_op jit(solution)/shard_map/ppermute | solution.py:18
  134.2 18.5 %collective-permute-start.26 = (f16[384,512]{1,0:T(8,128)(2,1)S(1)}, f16[384,512]{1,0:T(8,128)(2,1)S(1)}, u32[]{:S(2)}, u32[]{:S(2)}) collective-permute-start(f16[384,512]{1,0:T(8,128)(2,1)S(1)} %convert_element_type.44), channel_id=1, source_target_pairs={{0,18},{2,16},{16,2},{18,0},{1,19},{3,17},{17,3},{19,1},{4,22},{6,... | collective-permute-start | bytes 1179656 | tf_op jit(solution)/shard_map/ppermute | solution.py:22
  139.5 13.3 %collective-permute-start.27 = (f16[384,512]{1,0:T(8,128)(2,1)S(1)}, f16[384,512]{1,0:T(8,128)(2,1)S(1)}, u32[]{:S(2)}, u32[]{:S(2)}) collective-permute-start(f16[384,512]{1,0:T(8,128)(2,1)S(1)} %convert_element_type.46), channel_id=1, source_target_pairs={{0,2},{2,0},{1,3},{3,1},{4,6},{6,4},{5,7},{7,5},{8,10},{10,8},{9,1... | collective-permute-start | bytes 1179656 | tf_op jit(solution)/shard_map/ppermute | solution.py:18
  (21 other events, 82.9 us)
